TPU v7x, 512 devices: a whole 4x8x8 slice. The times are simulated.
512 devices in a mesh: section: 2 (over core), vocab: 64 (over z, x, y_lo), tok: 4 (over y_hi).
Axes of the slice: x: 4, y: 8 (y_hi: 4, y_lo: 2; y = y_hi * 2 + y_lo), z: 8, core: 2. Of those that a mesh axis runs over, the one named last changes fastest.
Arguments:
- rows: bfloat16 [2, 512, 3584], P('section', 'tok', 'vocab'), may hold values from -7 to 7
- targets: int32 [2, 512], P('section', 'tok'), may hold values from 0 to 65535
- proj_weight: bfloat16 [7168, 3584], P(None, 'vocab'), may hold values from -0.0625 to 0.0625
- head_weight: bfloat16 [3584, 65536], P(('section', 'tok'), 'vocab'), may hold values from -1 to 1
Outputs:
- head_grad: bfloat16 [3584, 65536], P(('section', 'tok'), 'vocab')
- hidden_grad: float32 [512, 3584], P('tok', 'vocab')
All inputs are finite; a program needn't handle non-finite values.
Results may differ from a plain program's by a relative error of at most 0.0052.
Values may be sent and summed in bfloat16 or wider, within the bound.
A program may use at most 64 MiB of HBM per device.

v0:
```python
import jax
import jax.numpy as jnp
from jax import lax
from jax.sharding import PartitionSpec as P

EPS = 1e-06
MTP_WEIGHT = 0.3


def shifted(value, axis, steps):
    count = lax.axis_size(axis)
    first, last = (max(0, -steps), min(count, count - steps))
    return lax.ppermute(value, axis, [(source, source + steps) for source in range(first, last)])


def normalize(inputs):
    values = inputs.astype(jnp.float32)
    inverse = lax.rsqrt(jnp.mean(values * values, axis=-1, keepdims=True) + EPS)
    return (values * inverse, inverse)


def local(rows, targets, proj_weight, head_weight):
    section_id = lax.axis_index("section")
    is_depth = section_id == 1
    own_cols = rows[0]
    col_count = own_cols.shape[1]
    model_width = col_count * lax.axis_size("vocab")
    col_start = lax.axis_index("vocab") * col_count
    relayed = shifted(own_cols, "section", 1)
    hidden_cols = jnp.where(is_depth, relayed, own_cols)
    hidden_full, embed_full = (
        lax.all_gather(hidden_cols, "vocab", axis=1, tiled=True),
        lax.all_gather(own_cols, "vocab", axis=1, tiled=True),
    )
    hidden_norm, hidden_inv = normalize(hidden_full)
    embed_norm = normalize(embed_full)[0]
    joined = jnp.concatenate([hidden_norm, embed_norm], axis=1).astype(jnp.bfloat16)
    projected = jnp.dot(joined, proj_weight, preferred_element_type=jnp.float32)
    mixed_rows = projected.astype(jnp.bfloat16)
    head_cols = jnp.where(is_depth, mixed_rows, own_cols)
    head_input = lax.all_gather(head_cols, "vocab", axis=1, tiled=True)
    normed, head_inv = normalize(head_input)
    rounded = normed.astype(jnp.bfloat16)
    weight_full = lax.all_gather(head_weight, ("section", "tok"), axis=0, tiled=True)
    logits = jnp.dot(rounded, weight_full, preferred_element_type=jnp.float32)
    row_max = lax.pmax(jnp.max(logits, axis=1), "vocab")
    denominator = lax.psum(jnp.sum(jnp.exp(logits - row_max[:, None]), axis=1), "vocab")
    probabilities = jnp.exp(logits - row_max[:, None]) / denominator[:, None]
    local_labels = targets[0] - lax.axis_index("vocab") * head_weight.shape[1]
    columns = lax.broadcasted_iota(jnp.int32, logits.shape, 1)
    onehot = (columns == local_labels[:, None]).astype(jnp.float32)
    weighting = jnp.where(is_depth, MTP_WEIGHT, 1.0)
    logit_grad = (weighting * (probabilities - onehot)).astype(jnp.bfloat16)
    pieces = weight_full
    feature_grad = lax.psum_scatter(
        lax.dot_general(
            pieces, logit_grad, (((1,), (1,)), ((), ())), preferred_element_type=jnp.float32
        ),
        "vocab",
        scatter_dimension=0,
        tiled=True,
    ).T
    normed_cols = lax.dynamic_slice_in_dim(normed, col_start, col_count, 1)
    rounded_cols = lax.dynamic_slice_in_dim(rounded, col_start, col_count, 1)
    row_dot = lax.psum(jnp.sum(feature_grad * rounded_cols.astype(jnp.float32), axis=1), "vocab")
    head_back = (feature_grad - normed_cols * (row_dot / model_width)[:, None]) * head_inv
    mixed_grad = head_back.astype(jnp.bfloat16)
    pieces = lax.slice_in_dim(proj_weight, 0, col_count * lax.axis_size("vocab"), axis=0)
    joined_grad = lax.psum_scatter(
        lax.dot_general(
            pieces, mixed_grad, (((1,), (1,)), ((), ())), preferred_element_type=jnp.float32
        ),
        "vocab",
        scatter_dimension=0,
        tiled=True,
    ).T
    hidden_norm_cols = lax.dynamic_slice_in_dim(hidden_norm, col_start, col_count, 1)
    joined_cols = lax.dynamic_slice_in_dim(joined, col_start, col_count, 1)
    hidden_dot = lax.psum(jnp.sum(joined_grad * joined_cols.astype(jnp.float32), axis=1), "vocab")
    depth_hidden = (
        joined_grad - hidden_norm_cols * (hidden_dot / model_width)[:, None]
    ) * hidden_inv
    own_grad = jnp.where(is_depth, depth_hidden, head_back)
    hidden_grad = lax.psum(own_grad, "section")
    token_blocks = lax.all_to_all(
        rounded, ("section", "tok"), split_axis=1, concat_axis=0, tiled=True
    )
    head_grad = lax.dot_general(
        token_blocks,
        lax.all_gather(logit_grad, ("section", "tok"), axis=0, tiled=True),
        (((0,), (0,)), ((), ())),
        preferred_element_type=jnp.float32,
    )
    return (head_grad.astype(jnp.bfloat16), hidden_grad)


def solution(mesh):
    placed = (
        P("section", "tok", "vocab"),
        P("section", "tok"),
        P(None, "vocab"),
        P(("section", "tok"), "vocab"),
    )
    return jax.shard_map(
        local,
        mesh=mesh,
        in_specs=placed,
        out_specs=(P(("section", "tok"), "vocab"), P("tok", "vocab")),
        check_vma=False,
    )
```

profile of v0, /device:TPU:1, one launch (start us, length us, event | category | flops | bytes accessed | tf_op | source)
XLA Modules:
  0.0 1819.2 jit_solution(2317213214801169858)
XLA Ops:
  7.2 0.7 all-gather.4.cloned.1.call-update
  7.9 1.3 collective-permute-start
  9.3 167.8 %all-gather = bf16[1,128,3584]{1,2,0:T(8,128)(2,1)S(1)} all-gather(bf16[1,128,56]{1,2,0:T(8,128)(2,1)} %param.4), channel_id=2, replica_groups=mesh['section'=2,'vocab'=64,'tok'=4] {'vocab'}, dimensions={2}, use_global_device_ids=true | all-gather | bytes 931840 | tf_op jit(solution)/shard_map/all_gather | solution.py:33
  177.1 0.5 fusion.3
  177.8 130.2 %all_gather.15 = bf16[128,3584]{0,1:T(8,128)(2,1)S(1)} all-gather(bf16[128,56]{0,1:T(8,128)(2,1)S(1)} %broadcast_select_fusion), channel_id=1, replica_groups=mesh['section'=2,'vocab'=64,'tok'=4] {'vocab'}, dimensions={1}, use_global_device_ids=true | all-gather | bytes 931840 | tf_op jit(solution)/shard_map/all_gather | solution.py:32
  308.1 0.5 fusion.1
  308.6 1.6 convert_multiply_fusion.4
  310.6 0.5 copy-done
  311.1 130.7 %all_gather.17 = bf16[128,3584]{0,1:T(8,128)(2,1)S(1)} all-gather(bf16[128,56]{0,1:T(8,128)(2,1)S(1)} %fusion.6), channel_id=1, replica_groups=mesh['section'=2,'vocab'=64,'tok'=4] {'vocab'}, dimensions={1}, use_global_device_ids=true | all-gather | bytes 931840 | tf_op jit(solution)/shard_map/all_gather | solution.py:41
  441.8 0.5 fusion.2
  442.3 0.5 copy-done.8
  442.8 1.8 convert_multiply_fusion.2
  444.6 4.6 fusion.23
  449.2 126.7 %pmax.7 = f32[128]{0:T(128)S(1)} all-reduce(f32[128]{0:T(128)S(1)} %get-tuple-element.6), channel_id=1, replica_groups=mesh['section'=2,'vocab'=64,'tok'=4] {'vocab'}, use_global_device_ids=true, to_apply=%region_4.5 | all-reduce | flops 128 | bytes 1024 | tf_op jit(solution)/shard_map/pmax | solution.py:46
  576.1 127.0 %psum.28 = f32[128]{0:T(128)S(1)} all-reduce(f32[128]{0:T(128)S(1)} %fusion.9), channel_id=1, replica_groups=mesh['section'=2,'vocab'=64,'tok'=4] {'vocab'}, use_global_device_ids=true, to_apply=%region_6.7 | all-reduce | flops 128 | bytes 1024 | tf_op jit(solution)/shard_map/psum | solution.py:47
  703.4 5.7 convolution_bitcast_fusion.1
  709.1 1.7 copy.12
  710.9 0.7 all-gather.6.cloned.1.call-update
  711.6 409.8 %reduce-scatter.9.cloned.1.call-done = f32[56,128]{1,0:T(8,128)} async-done(((f32[3584,128]{1,0:T(8,128)}), f32[56,128]{1,0:T(8,128)}) %reduce-scatter.9.cloned.1.call-update) | async-done | bytes 28688
  1121.4 0.8 fusion.16
  1122.1 128.8 %psum.29 = f32[128]{0:T(128)S(1)} all-reduce(f32[128]{0:T(128)S(1)} %fusion.16), channel_id=1, replica_groups=mesh['section'=2,'vocab'=64,'tok'=4] {'vocab'}, use_global_device_ids=true, to_apply=%region_9.10 | all-reduce | flops 128 | bytes 1024 | tf_op jit(solution)/shard_map/psum | solution.py:65
  1251.0 0.5 copy-done.10
  1251.5 1.2 convolution_bitcast_fusion
  1252.7 1.7 copy.13
  1254.4 82.1 %all-to-all-start = ((bf16[128,8,448]{0,2,1:T(8,128)(2,1)}), bf16[128,8,448]{0,2,1:T(8,128)(2,1)S(1)}, u32[]{:S(2)}, u32[]{:S(2)}) async-start(bf16[128,8,448]{0,2,1:T(8,128)(2,1)} %bitcast.3), calls=%async_computation | async-start | bytes 1835008 | tf_op jit(solution)/shard_map/all_to_all | solution.py:85
  1336.5 27.2 %all-to-all-done = bf16[128,8,448]{0,2,1:T(8,128)(2,1)S(1)} async-done(((bf16[128,8,448]{0,2,1:T(8,128)(2,1)}), bf16[128,8,448]{0,2,1:T(8,128)(2,1)S(1)}, u32[]{:S(2)}, u32[]{:S(2)}) %all-to-all-start) | async-done | bytes 917536 | tf_op jit(solution)/shard_map/all_to_all | solution.py:85
  1363.7 3.6 convolution_convert_fusion
  1367.3 232.0 %reduce-scatter.11.cloned.1.call-done = f32[56,128]{1,0:T(8,128)} async-done(((f32[3584,128]{1,0:T(8,128)}), f32[56,128]{1,0:T(8,128)}) %reduce-scatter.11.cloned.1.call-update) | async-done | bytes 28688
  1599.3 0.9 fusion.13
  1600.2 129.5 %psum.30 = f32[128]{0:T(128)S(1)} all-reduce(f32[128]{0:T(128)S(1)} %fusion.13), channel_id=1, replica_groups=mesh['section'=2,'vocab'=64,'tok'=4] {'vocab'}, use_global_device_ids=true, to_apply=%region_12.13 | all-reduce | flops 128 | bytes 1024 | tf_op jit(solution)/shard_map/psum | solution.py:79
  1729.8 0.8 fusion.15
  1730.5 82.1 %psum.31 = f32[128,56]{0,1:T(8,128)} all-reduce(f32[128,56]{0,1:T(8,128)S(1)} %fusion.15), channel_id=1, replica_groups=mesh['section'=2,'vocab'=64,'tok'=4] {'section'}, use_global_device_ids=true, to_apply=%region_13.14 | all-reduce | flops 7168 | bytes 57344 | tf_op jit(solution)/shard_map/psum | solution.py:84
  (47 shorter events, 1.4 us)
Async XLA Ops:
  7.2 437.4 %all-gather.4.cloned.1.call-start = ((), (), s32[]{:S(2)}) async-start(), calls=%async_computation.3 | async-start | bytes 8257536 | tf_op jit(solution)/shard_map/all_gather | solution.py:44
  7.9 1113.5 %reduce-scatter.9.cloned.1.call-start = ((), (), s32[]{:S(2)}) async-start(), calls=%async_computation.5 | async-start | bytes 1863680
  7.9 169.9 %collective-permute-start = (bf16[128,56]{0,1:T(8,128)(2,1)}, bf16[128,56]{0,1:T(8,128)(2,1)S(1)}, u32[]{:S(2)}, u32[]{:S(2)}) collective-permute-start(bf16[128,56]{0,1:T(8,128)(2,1)} %bitcast.50), channel_id=1, source_target_pairs={{0,256},{1,257},{2,258},{3,259},{4,260},{5,261},{6,262},{7,263},{8... | collective-permute-start | bytes 43016 | tf_op jit(solution)/shard_map/ppermute | solution.py:13
  9.2 168.5 %copy-start.14 = (s32[1,128]{1,0:T(1,128)S(1)}, s32[1,128]{1,0:T(1,128)}, u32[]{:S(2)}) copy-start(s32[1,128]{1,0:T(1,128)} %param.5) | copy-start | bytes 1540
  9.3 168.6 %copy-start.7 = (bf16[1,128,56]{1,2,0:T(8,128)(2,1)S(1)}, bf16[1,128,56]{1,2,0:T(8,128)(2,1)}, u32[]{:S(2)}) copy-start(bf16[1,128,56]{1,2,0:T(8,128)(2,1)} %param.4) | copy-start | bytes 43012
  308.6 1.6 copy-start.12
  308.6 1.6 copy-start.4
  310.1 0.9 copy-start
  442.3 0.5 copy-start.8
  703.4 5.7 copy-start.2
  710.8 540.7 %copy-start.5 = (bf16[7168,56]{0,1:T(8,128)(2,1)S(1)}, bf16[7168,56]{0,1:T(8,128)(2,1)}, u32[]{:S(2)}) copy-start(bf16[7168,56]{0,1:T(8,128)(2,1)} %param.6) | copy-start | bytes 2408452
  710.8 652.9 %all-gather.6.cloned.1.call-start = ((), (), s32[]{:S(2)}) async-start(), calls=%async_computation.4 | async-start | bytes 2359296 | tf_op jit(solution)/shard_map/all_gather | solution.py:90
  711.5 887.8 %reduce-scatter.11.cloned.1.call-start = ((), (), s32[]{:S(2)}) async-start(), calls=%async_computation.6 | async-start | bytes 1863680
  1251.0 0.5 copy-start.10
  1254.4 109.2 %all-to-all-start = ((bf16[128,8,448]{0,2,1:T(8,128)(2,1)}), bf16[128,8,448]{0,2,1:T(8,128)(2,1)S(1)}, u32[]{:S(2)}, u32[]{:S(2)}) async-start(bf16[128,8,448]{0,2,1:T(8,128)(2,1)} %bitcast.3), calls=%async_computation | async-start | bytes 1835008 | tf_op jit(solution)/shard_map/all_to_all | solution.py:85
  1336.5 262.8 %copy-start.1 = (bf16[128,3584]{0,1:T(8,128)(2,1)S(1)}, bf16[128,3584]{0,1:T(8,128)(2,1)}, u32[]{:S(2)}) copy-start(bf16[128,3584]{0,1:T(8,128)(2,1)} %copy-done) | copy-start | bytes 2752516
  1367.3 362.4 %copy-start.3 = (f32[56,128]{1,0:T(8,128)S(1)}, f32[56,128]{1,0:T(8,128)}, u32[]{:S(2)}) copy-start(f32[56,128]{1,0:T(8,128)} %reduce-scatter.9.cloned.1.call-done) | copy-start | bytes 86020
  1367.3 362.4 %copy-start.9 = (f32[128]{0:T(128)S(1)}, f32[128]{0:T(128)}, u32[]{:S(2)}) copy-start(f32[128]{0:T(128)} %copy-done.8) | copy-start | bytes 1540
  1367.3 362.4 %copy-start.11 = (f32[128]{0:T(128)S(1)}, f32[128]{0:T(128)}, u32[]{:S(2)}) copy-start(f32[128]{0:T(128)} %copy-done.10) | copy-start | bytes 1540
  1367.3 362.4 %copy-start.13 = (f32[128]{0:T(128)S(1)}, f32[128]{0:T(128)}, u32[]{:S(2)}) copy-start(f32[128]{0:T(128)} %copy-done.12) | copy-start | bytes 1540
  1599.3 130.4 %copy-start.6 = (f32[56,128]{1,0:T(8,128)S(1)}, f32[56,128]{1,0:T(8,128)}, u32[]{:S(2)}) copy-start(f32[56,128]{1,0:T(8,128)} %reduce-scatter.11.cloned.1.call-done) | copy-start | bytes 86020
Sparse Core Ops, SparseCore 0:
  10.2 92.8 all-gather.3
  710.9 410.4 reduce-scatter.8
  1123.8 83.5 all-gather.5
  1254.6 344.6 reduce-scatter.10
where the time goes:
time: 1820 us
  blocking collectives  1020 us (56%)
  waiting for transfers between devices  670 us (37%)
  starting transfers between devices  83.5 us (5%)
    unnamed x6, waiting for transfers between devices  643 us
    all_gather x1, blocking collectives, local(): lax.all_gather(own_cols, 'vocab', axis=1, tiled=True)  168 us
    all_gather x1, blocking collectives, local(): head_input = lax.all_gather(head_cols, 'vocab', axis=1, tiled=True)  131 us
    all_gather x1, blocking collectives, local(): lax.all_gather(hidden_cols, 'vocab', axis=1, tiled=True)  130 us
    psum x1, blocking collectives, local(): lax.psum(jnp.sum(joined_grad * joined_cols.astype(jnp.float32), axis=1),...  130 us
    psum x1, blocking collectives, local(): lax.psum(jnp.sum(feature_grad * rounded_cols.astype(jnp.float32), axis=1)...  129 us
    psum x1, blocking collectives, local(): lax.psum(jnp.sum(jnp.exp(logits - row_max[:, None]), axis=1), 'vocab')  127 us
    pmax x1, blocking collectives, local(): row_max = lax.pmax(jnp.max(logits, axis=1), 'vocab')  127 us
  transfers between devices with their start and end apart: 6, of which 3 were waited for; matrix products, arithmetic and copies ran while one was open for 1% of the time, Pallas kernels for 0%

commit v1 on v0

v1 whole, which is shorter than its diff:
```python
import jax
import jax.numpy as jnp
from jax import lax
from jax.experimental import pallas as pl
from jax.experimental.pallas import tpu as pltpu
from jax.sharding import PartitionSpec as P

EPS = 1e-06
MTP_WEIGHT = 0.3
D = 3584
T = 128
C = 56
CP = 64
VS = 1024
KB = 448
MESH = pl.DeviceIdType.MESH
BF = jnp.bfloat16
F32 = jnp.float32


def rcopy(src, dst, ssem, rsem, dev):
    copy = pltpu.make_async_remote_copy(
        src_ref=src, dst_ref=dst, send_sem=ssem, recv_sem=rsem, device_id=dev, device_id_type=MESH
    )
    copy.start()


def await_bytes(ref, sem):
    pltpu.make_async_copy(ref, ref, sem).wait()


def kernel(
    rows_ref, lab_ref, proj_ref, w_ref, hg_ref, out_ref,
    wf, proj, ga, gb, normed, rt, rnd, logt, lg_all, r_all,
    p3, rx3, az3, af3, rz3, by3, ry3,
    p4, rx4, az4, af4, rz4, by4, ry4,
    sx, sz, sy, hx, hz, hy,
    xch, xin, bk, bkin,
    loc_sem, w_s, w_r, l_s, l_r, r_s, r_r,
    g1s, g1r, g2s, g2r, st_s, st_r, h_s, h_r, q3s, q3r, q4s, q4r, x_s, x_r,
):
    s = lax.axis_index("section")
    v = lax.axis_index("vocab")
    t = lax.axis_index("tok")
    z = lax.div(v, 8)
    x = lax.rem(lax.div(v, 2), 4)
    yl = lax.rem(v, 2)
    b = s * 4 + t
    sib = {"section": 1 - s}
    t_right = lax.rem(t + 1, 4)
    t_left = lax.rem(t + 3, 4)
    t_far = lax.rem(t + 2, 4)

    def at_z(d):
        return {"vocab": lax.rem(z + d, 8) * 8 + x * 2 + yl}

    def at_x(d):
        return {"vocab": z * 8 + lax.rem(x + d, 4) * 2 + yl}

    at_y = {"vocab": z * 8 + x * 2 + (1 - yl)}

    barrier = pltpu.get_barrier_semaphore()
    for d in range(1, 8):
        pl.semaphore_signal(barrier, inc=1, device_id=at_z(d), device_id_type=MESH)
    for d in range(1, 4):
        pl.semaphore_signal(barrier, inc=1, device_id=at_x(d), device_id_type=MESH)
    pl.semaphore_signal(barrier, inc=1, device_id=at_y, device_id_type=MESH)
    for d in range(1, 8):
        o = lax.rem(b + d, 8)
        pl.semaphore_signal(
            barrier, inc=1, device_id={"section": lax.div(o, 4), "tok": lax.rem(o, 4)}, device_id_type=MESH
        )
    ga[z, x, yl] = rows_ref[...]
    pl.semaphore_wait(barrier, 18)

    def gather(g, ss, rs):
        rcopy(g.at[z, x, yl], g.at[z, x, yl], ss.at[0], rs.at[0], at_y)
        await_bytes(g.at[z, x, 1 - yl], rs.at[0])
        for d in (4, 3, 5, 2, 6, 1, 7):
            rcopy(g.at[z, x], g.at[z, x], ss.at[1], rs.at[1], at_z(d))
        await_bytes(g.at[pl.ds(0, 7), x], rs.at[1])
        xl = lax.rem(x + 3, 4)
        xr = lax.rem(x + 1, 4)
        rcopy(g.at[:, x], g.at[:, x], ss.at[2], rs.at[2], at_x(1))
        rcopy(g.at[:, x], g.at[:, x], ss.at[2], rs.at[3], at_x(3))
        await_bytes(g.at[:, xl], rs.at[2])
        lo = pl.ds(0, 4)
        hi = pl.ds(4, 4)
        rcopy(g.at[lo, xl], g.at[lo, xl], ss.at[2], rs.at[4], at_x(1))
        await_bytes(g.at[:, xr], rs.at[3])
        rcopy(g.at[hi, xr], g.at[hi, xr], ss.at[2], rs.at[5], at_x(3))
        await_bytes(g.at[lo, x], rs.at[4])
        await_bytes(g.at[hi, x], rs.at[5])

    def gather_sent(g, ss):
        await_bytes(g.at[z, x, yl], ss.at[0])
        await_bytes(g.at[pl.ds(0, 7), x], ss.at[1])
        await_bytes(g.at[:, pl.ds(0, 3)], ss.at[2])

    def ring_start(own, piece, ss, rs):
        right = {"tok": t_right}
        left = {"tok": t_left}
        rcopy(own(0), piece(b, 0), ss, rs.at[0], right)
        rcopy(own(1), piece(b, 1), ss, rs.at[3], left)
        rcopy(own(0), piece(b, 0), ss, rs.at[6], sib)
        rcopy(own(1), piece(b, 1), ss, rs.at[6], sib)
        rcopy(own(1), piece(b, 1), ss, rs.at[1], right)
        rcopy(own(0), piece(b, 0), ss, rs.at[2], left)

    def hand(piece, blk, h, ss, rs):
        rcopy(piece(blk, h), piece(blk, h), ss, rs.at[6], sib)

    def ring_mid(piece, ss, rs):
        bl = s * 4 + t_left
        br = s * 4 + t_right
        await_bytes(piece(bl, 0), rs.at[0])
        rcopy(piece(bl, 0), piece(bl, 0), ss, rs.at[4], {"tok": t_right})
        await_bytes(piece(br, 1), rs.at[3])
        rcopy(piece(br, 1), piece(br, 1), ss, rs.at[5], {"tok": t_left})
        hand(piece, bl, 0, ss, rs)
        hand(piece, br, 1, ss, rs)

    def ring_late(piece, ss, rs):
        bl = s * 4 + t_left
        br = s * 4 + t_right
        bf = s * 4 + t_far
        await_bytes(piece(bl, 1), rs.at[1])
        hand(piece, bl, 1, ss, rs)
        await_bytes(piece(br, 0), rs.at[2])
        hand(piece, br, 0, ss, rs)
        await_bytes(piece(bf, 0), rs.at[4])
        hand(piece, bf, 0, ss, rs)
        await_bytes(piece(bf, 1), rs.at[5])
        hand(piece, bf, 1, ss, rs)

    def w_own(h):
        return w_ref.at[pl.ds(224 * h, 224), :]

    def w_piece(blk, h):
        return wf.at[pl.ds(pl.multiple_of(KB * blk + 224 * h, 32), 224), :]

    def l_piece(blk, h):
        return lg_all.at[pl.ds(512 * h, 512), pl.ds(pl.multiple_of(blk * T, T), T)]

    def l_own(h):
        return l_piece(b, h)

    pcopy = pltpu.make_async_copy(proj_ref, proj, loc_sem.at[0])
    pcopy.start()
    ring_start(w_own, w_piece, w_s, w_r)
    wcopy = pltpu.make_async_copy(w_ref, wf.at[pl.ds(pl.multiple_of(KB * b, 64), KB), :], loc_sem.at[1])
    wcopy.start()

    def normalize(g):
        def add(i, acc):
            for j in range(8):
                blk = g[i, j // 2, j % 2][:C, :].astype(F32)
                acc = acc + (blk * blk)
            return acc

        total = lax.fori_loop(0, 8, add, jnp.zeros((C, T), F32))
        inv = lax.rsqrt(jnp.sum(total, axis=0, keepdims=True) * (1.0 / D) + EPS)

        def scale(i, carry):
            parts = [g[i, j // 2, j % 2][:C, :].astype(F32) for j in range(8)]
            block = jnp.concatenate(parts, axis=0) * inv
            r = pl.multiple_of(i * KB, KB)
            normed[pl.ds(r, KB), :] = block
            rt[pl.ds(r, KB), :] = block.astype(BF)
            return carry

        lax.fori_loop(0, 8, scale, 0)
        return inv

    gather(ga, g1s, g1r)
    inv1 = normalize(ga)
    pcopy.wait()
    part = lax.dot_general(
        proj[pl.ds(pl.multiple_of(s * D, D), D), :], rt[...], (((0,), (0,)), ((), ())),
        preferred_element_type=F32,
    )
    own_rows = pl.ds(pl.multiple_of(v * C, 8), C)

    @pl.when(s == 0)
    def _():
        xch[pl.ds(0, C), :] = part
        xch[pl.ds(C, 8), :] = jnp.broadcast_to(inv1, (8, T))
        xch[pl.ds(CP, C), :] = normed[own_rows, :]
        xch[pl.ds(CP + C, 8), :] = jnp.zeros((8, T), F32)
        rcopy(xch, xin, x_s.at[0], x_r.at[0], sib)
        sy[2] = jnp.broadcast_to(inv1, (8, T))
        ring_mid(w_piece, w_s, w_r)

    @pl.when(s == 1)
    def _():
        await_bytes(xin, x_r.at[0])
        mixed = part + xin[pl.ds(0, C), :]
        gb[z, x, yl] = jnp.concatenate([mixed, jnp.zeros((CP - C, T), F32)], axis=0).astype(BF)
        gather(gb, g2s, g2r)
        sy[2] = jnp.broadcast_to(normalize(gb), (8, T))
        ring_mid(w_piece, w_s, w_r)

    def turn(i, carry):
        r = pl.multiple_of(i * T, T)
        rnd[:, pl.ds(r, T)] = normed[pl.ds(r, T), :].T.astype(BF)
        return carry

    lax.fori_loop(0, D // T, turn, 0)
    ring_late(w_piece, w_s, w_r)
    wcopy.wait()
    await_bytes(wf.at[pl.ds(0, 4 * KB), :], w_r.at[6])

    def to_owner(d, carry):
        o = lax.rem(b + d, 8)
        rcopy(
            rt.at[pl.ds(pl.multiple_of(o * KB, 64), KB), :],
            r_all.at[:, pl.ds(pl.multiple_of(b * T, T), T)],
            r_s, r_r, {"section": lax.div(o, 4), "tok": lax.rem(o, 4)},
        )
        return carry

    def logits_tile(i, carry):
        r = pl.multiple_of(i * 256, 256)
        tile = jnp.dot(rnd[...], wf[:, pl.ds(r, 256)], preferred_element_type=F32)
        logt[pl.ds(r, 256), :] = tile.T
        return carry

    lax.fori_loop(0, 4, logits_tile, 0)
    r_all[:, pl.ds(pl.multiple_of(b * T, T), T)] = rt[pl.ds(pl.multiple_of(b * KB, 64), KB), :]

    label = lab_ref[...]
    place = lax.broadcasted_iota(jnp.int32, (VS, T), 0)
    hit = place == label
    values = logt[...]
    top = jnp.max(values, axis=0, keepdims=True)
    expo = jnp.exp(values - top)
    den = jnp.sum(expo, axis=0, keepdims=True)
    sel = jnp.sum(expo * values, axis=0, keepdims=True)
    lab = jnp.sum(jnp.where(hit, values, 0.0), axis=0, keepdims=True)

    def combine(slots):
        m = slots[0][0:1]
        for q in slots[1:]:
            m = jnp.maximum(m, q[0:1])
        d_ = jnp.zeros((1, T), F32)
        e_ = jnp.zeros((1, T), F32)
        l_ = jnp.zeros((1, T), F32)
        for q in slots:
            f = jnp.exp(q[0:1] - m)
            d_ = d_ + q[1:2] * f
            e_ = e_ + q[2:3] * f
            l_ = l_ + q[3:4]
        return jnp.concatenate([m, d_, e_, l_, jnp.zeros((4, T), F32)], axis=0)

    sx[x] = jnp.concatenate([top, den, sel, lab, jnp.zeros((4, T), F32)], axis=0)
    for d in (2, 1, 3):
        rcopy(sx.at[x], sx.at[x], st_s.at[0], st_r.at[0], at_x(d))
    await_bytes(sx.at[pl.ds(0, 3)], st_r.at[0])
    sz[z] = combine([sx[i] for i in range(4)])
    for d in (4, 3, 5, 2, 6, 1, 7):
        rcopy(sz.at[z], sz.at[z], st_s.at[1], st_r.at[1], at_z(d))
    await_bytes(sz.at[pl.ds(0, 7)], st_r.at[1])
    sy[yl] = combine([sz[i] for i in range(8)])
    rcopy(sy.at[yl], sy.at[yl], st_s.at[2], st_r.at[2], at_y)
    await_bytes(sy.at[1 - yl], st_r.at[2])
    stats = combine([sy[0], sy[1]])
    weighting = jnp.where(s == 1, MTP_WEIGHT, 1.0).astype(F32)
    inv_den = 1.0 / stats[1:2]
    mean_dot = weighting * (stats[2:3] * inv_den - stats[3:4]) * (1.0 / D)
    prob = jnp.exp(logt[...] - stats[0:1]) * inv_den
    lgt = (weighting * (prob - hit.astype(F32))).astype(BF)
    lg_all[:, pl.ds(pl.multiple_of(b * T, T), T)] = lgt
    ring_start(l_own, l_piece, l_s, l_r)

    pad = jnp.zeros((CP - C, T), F32)

    def spread(block, p, i):
        for j in range(8):
            p[i, j // 2, j % 2] = jnp.concatenate([block[C * j:C * (j + 1), :], pad], axis=0).astype(BF)

    def feature(i, carry):
        r = pl.multiple_of(i * KB, KB)
        block = jnp.dot(wf[pl.ds(r, KB), :], lgt, preferred_element_type=F32)
        spread(block, p3, i)
        return carry

    lax.fori_loop(0, 8, feature, 0)

    def scatter(p, rx, az, af, rz, by, ry, ss, rs):
        for d in (2, 1, 3):
            xo = lax.rem(x + d, 4)
            rcopy(p.at[:, xo], rx.at[x], ss.at[0], rs.at[0], at_x(d))

        def rest():
            await_bytes(rx.at[pl.ds(0, 3)], rs.at[0])

            def add(i, carry):
                for j in range(2):
                    a = p[i, x, j].astype(F32)
                    for d in range(1, 4):
                        a = a + rx[lax.rem(x + d, 4), i, j].astype(F32)
                    af[i, j] = a
                    az[i, j] = a.astype(BF)
                return carry

            lax.fori_loop(0, 8, add, 0)
            for d in (4, 3, 5, 2, 6, 1, 7):
                zo = lax.rem(z + d, 8)
                rcopy(az.at[zo], rz.at[z], ss.at[1], rs.at[1], at_z(d))
            await_bytes(rz.at[pl.ds(0, 7)], rs.at[1])
            for j in range(2):
                a = af[z, j]
                for d in range(1, 8):
                    a = a + rz[lax.rem(z + d, 8), j].astype(F32)
                by[j] = a
            rcopy(by.at[1 - yl], ry, ss.at[2], rs.at[2], at_y)
            await_bytes(ry, rs.at[2])
            return (by[yl] + ry[...])[:C, :]

        return rest

    def scatter_sent(rx, rz, ry, ss):
        await_bytes(rx.at[pl.ds(0, 3)], ss.at[0])
        await_bytes(rz.at[pl.ds(0, 7)], ss.at[1])
        await_bytes(ry, ss.at[2])

    rest = scatter(p3, rx3, az3, af3, rz3, by3, ry3, q3s, q3r)
    lax.fori_loop(1, 8, to_owner, 0)
    fgrad = rest()
    back = (fgrad - normed[own_rows, :] * mean_dot) * sy[2][0:1]

    def head_grad():
        await_bytes(r_all.at[:, pl.ds(0, 7 * T)], r_r)
        ring_late(l_piece, l_s, l_r)
        await_bytes(lg_all.at[:, pl.ds(0, 4 * T)], l_r.at[6])

        def tile(i, carry):
            r = pl.multiple_of(i * 256, 256)
            g = lax.dot_general(
                r_all[...], lg_all[pl.ds(r, 256), :], (((1,), (1,)), ((), ())), preferred_element_type=F32
            )
            hg_ref[:, pl.ds(r, 256)] = g.astype(BF)
            return carry

        lax.fori_loop(0, 4, tile, 0)

    @pl.when(s == 0)
    def _():
        bk[...] = back
        rcopy(bk, bkin, x_s.at[1], x_r.at[1], sib)
        ring_mid(l_piece, l_s, l_r)
        head_grad()
        await_bytes(bkin, x_r.at[1])
        out_ref[...] = back + bkin[...]
        await_bytes(xch, x_s.at[0])

    @pl.when(s == 1)
    def _():
        mg = back.astype(BF)

        def joined(i, carry):
            r = pl.multiple_of(i * KB, KB)
            block = jnp.dot(proj[pl.ds(r, KB), :], mg, preferred_element_type=F32)
            spread(block, p4, i)
            return carry

        lax.fori_loop(0, 8, joined, 0)
        rest4 = scatter(p4, rx4, az4, af4, rz4, by4, ry4, q4s, q4r)
        hdot = jnp.sum(mg.astype(F32) * xin[pl.ds(0, C), :], axis=0, keepdims=True)
        hx[x] = jnp.broadcast_to(hdot, (8, T))
        for d in (2, 1, 3):
            rcopy(hx.at[x], hx.at[x], h_s.at[0], h_r.at[0], at_x(d))
        ring_mid(l_piece, l_s, l_r)
        await_bytes(hx.at[pl.ds(0, 3)], h_r.at[0])
        hz[z] = hx[0] + hx[1] + hx[2] + hx[3]
        for d in (4, 3, 5, 2, 6, 1, 7):
            rcopy(hz.at[z], hz.at[z], h_s.at[1], h_r.at[1], at_z(d))
        jgrad = rest4()
        await_bytes(hz.at[pl.ds(0, 7)], h_r.at[1])
        tot = hz[0]
        for i in range(1, 8):
            tot = tot + hz[i]
        hy[yl] = tot
        rcopy(hy.at[yl], hy.at[yl], h_s.at[2], h_r.at[2], at_y)
        await_bytes(hy.at[1 - yl], h_r.at[2])
        hmean = (hy[0] + hy[1])[0:1] * (1.0 / D)
        depth = (jgrad - xin[pl.ds(CP, C), :] * hmean) * xin[pl.ds(C, 1), :]
        bk[...] = depth
        rcopy(bk, bkin, x_s.at[1], x_r.at[1], sib)
        await_bytes(bkin, x_r.at[1])
        out_ref[...] = bkin[...] + depth
        head_grad()
        gather_sent(gb, g2s)
        scatter_sent(rx4, rz4, ry4, q4s)
        await_bytes(hx.at[pl.ds(0, 3)], h_s.at[0])
        await_bytes(hz.at[pl.ds(0, 7)], h_s.at[1])
        await_bytes(hy.at[0], h_s.at[2])

    await_bytes(bk, x_s.at[1])
    gather_sent(ga, g1s)
    scatter_sent(rx3, rz3, ry3, q3s)
    await_bytes(sx.at[pl.ds(0, 3)], st_s.at[0])
    await_bytes(sz.at[pl.ds(0, 7)], st_s.at[1])
    await_bytes(sy.at[0], st_s.at[2])
    await_bytes(r_all.at[:, pl.ds(0, 7 * T)], r_s)
    await_bytes(wf.at[pl.ds(0, 7 * KB), :], w_s)
    await_bytes(lg_all.at[:, pl.ds(0, 7 * T)], l_s)


def local(rows, targets, proj_weight, head_weight):
    rows_t = jnp.pad(rows[0].T, ((0, CP - C), (0, 0)))
    labels = targets - lax.axis_index("vocab") * VS
    vm = pl.BlockSpec(memory_space=pltpu.VMEM)
    anyspace = pl.BlockSpec(memory_space=pl.ANY)
    dma = pltpu.SemaphoreType.DMA

    def rs_bufs():
        return [
            pltpu.VMEM((8, 4, 2, CP, T), BF),
            pltpu.VMEM((4, 8, 2, CP, T), BF),
            pltpu.VMEM((8, 2, CP, T), BF),
            pltpu.VMEM((8, 2, CP, T), F32),
            pltpu.VMEM((8, 2, CP, T), BF),
            pltpu.VMEM((2, CP, T), F32),
            pltpu.VMEM((CP, T), F32),
        ]

    head_grad, grad_t = pl.pallas_call(
        kernel,
        out_shape=(
            jax.ShapeDtypeStruct((KB, VS), BF),
            jax.ShapeDtypeStruct((C, T), F32),
        ),
        in_specs=[vm, vm, anyspace, anyspace],
        out_specs=(vm, vm),
        scratch_shapes=[
            pltpu.VMEM((D, VS), BF),
            pltpu.VMEM((2 * D, C), BF),
            pltpu.VMEM((8, 4, 2, CP, T), BF),
            pltpu.VMEM((8, 4, 2, CP, T), BF),
            pltpu.VMEM((D, T), F32),
            pltpu.VMEM((D, T), BF),
            pltpu.VMEM((T, D), BF),
            pltpu.VMEM((VS, T), F32),
            pltpu.VMEM((VS, 8 * T), BF),
            pltpu.VMEM((KB, 8 * T), BF),
            *rs_bufs(),
            *rs_bufs(),
            pltpu.VMEM((4, 8, T), F32),
            pltpu.VMEM((8, 8, T), F32),
            pltpu.VMEM((3, 8, T), F32),
            pltpu.VMEM((4, 8, T), F32),
            pltpu.VMEM((8, 8, T), F32),
            pltpu.VMEM((2, 8, T), F32),
            pltpu.VMEM((2 * CP, T), F32),
            pltpu.VMEM((2 * CP, T), F32),
            pltpu.VMEM((C, T), F32),
            pltpu.VMEM((C, T), F32),
            dma((2,)), dma, dma((7,)), dma, dma((7,)), dma, dma,
            dma((3,)), dma((6,)), dma((3,)), dma((6,)),
            dma((3,)), dma((3,)), dma((3,)), dma((3,)),
            dma((3,)), dma((3,)), dma((3,)), dma((3,)),
            dma((2,)), dma((2,)),
        ],
        compiler_params=pltpu.CompilerParams(
            collective_id=0, has_side_effects=True, vmem_limit_bytes=56 * 1024 * 1024
        ),
        cost_estimate=pl.CostEstimate(flops=3 * 10**9, bytes_accessed=2 * 10**7, transcendentals=3 * 10**5),
        name="head",
    )(rows_t, labels, proj_weight, head_weight)
    return head_grad, grad_t.T


def solution(mesh):
    placed = (
        P("section", "tok", "vocab"),
        P("section", "tok"),
        P(None, "vocab"),
        P(("section", "tok"), "vocab"),
    )
    return jax.shard_map(
        local,
        mesh=mesh,
        in_specs=placed,
        out_specs=(P(("section", "tok"), "vocab"), P("tok", "vocab")),
        check_vma=False,
    )
```

time: 1820 us -> 184 us (0.10)
  the two profiles are of different devices: /device:TPU:1 before, /device:TPU:48 now
where the time goes in v1:
time: 184 us
  Pallas kernels  175 us (95%)
  local copies, waits for them, and re-layouts  6.69 us (4%)
    pallas_call x1, Pallas kernels, local(): pl.pallas_call(kernel, out_shape=(jax.ShapeDtypeStruct((KB, VS), BF), jax...  175 us
    unnamed x5, local copies, waits for them, and re-layouts  5.37 us

profile of v1, /device:TPU:48, one launch (start us, length us, event | category | flops | bytes accessed | tf_op | source)
XLA Modules:
  0.0 183.9 jit_solution(6201558482169276792)
XLA Ops:
  0.6 1.2 broadcast_subtract_fusion.lab_ref
  1.8 1.3 pad.4.rows_ref
  3.1 2.6 %copy.6.proj_ref = bf16[7168,56]{1,0:T(8,128)(2,1)} copy(bf16[7168,56]{0,1:T(8,128)(2,1)} %param.6) | data formatting | bytes 1605632 | tf_op args[2]
  5.7 175.4 %head.1 = (bf16[448,1024]{1,0:T(8,128)(2,1)}, f32[56,128]{1,0:T(8,128)}) custom-call(bf16[64,128]{1,0:T(8,128)(2,1)} %pad.4.rows_ref, s32[1,128]{1,0:T(1,128)} %broadcast_subtract_fusion.lab_ref, bf16[7168,56]{1,0:T(8,128)(2,1)} %copy.6.proj_ref, bf16[448,1024]{1,0:T(8,128)(2,1)} %w_ref.1), custom_call_target="tpu_custom_call" | custom-call | flops 3000000000 | bytes 20000000 | tf_op jit(solution)/shard_map/head/pallas_call | solution.py:428
  181.1 0.0 copy-start
  181.1 2.2 %copy.9 = bf16[448,1024]{1,0:T(8,128)(2,1)} copy(bf16[448,1024]{1,0:T(8,128)(2,1)} %get-tuple-element.8) | data formatting | bytes 1835008
  183.3 0.0 copy-done
  183.3 0.6 copy.10
Async XLA Ops:
  181.1 2.2 %copy-start = (f32[56,128]{1,0:T(8,128)S(1)}, f32[56,128]{1,0:T(8,128)}, u32[]{:S(2)}) copy-start(f32[56,128]{1,0:T(8,128)} %get-tuple-element.5) | copy-start | bytes 86020

commit v2 on v1

--- a/solution.py
+++ b/solution.py
@@ -14,6 +14,9 @@
 VS = 1024
 KB = 448
 MESH = pl.DeviceIdType.MESH
+ORDER = (8, 7, 9, 6, 10, 5, 11, 4, 12, 3, 13, 2, 14, 1, 15)
+GROUP = 2
+GROUPS = 8 // GROUP
 BF = jnp.bfloat16
 F32 = jnp.float32
 
@@ -31,10 +34,10 @@
 
 def kernel(
     rows_ref, lab_ref, proj_ref, w_ref, hg_ref, out_ref,
-    wf, proj, ga, gb, normed, rt, rnd, logt, lg_all, r_all,
-    p3, rx3, az3, af3, rz3, by3, ry3,
-    p4, rx4, az4, af4, rz4, by4, ry4,
-    sx, sz, sy, hx, hz, hy,
+    wf, proj, ph, ga, gb, normed, rt, rnd, logt, lg_all, r_all,
+    p3, rx3, az3, af3, rz3,
+    p4, rx4, az4, af4, rz4,
+    sx, sz, inv_keep, hx, hz,
     xch, xin, bk, bkin,
     loc_sem, w_s, w_r, l_s, l_r, r_s, r_r,
     g1s, g1r, g2s, g2r, st_s, st_r, h_s, h_r, q3s, q3r, q4s, q4r, x_s, x_r,
@@ -57,25 +60,35 @@
     def at_x(d):
         return {"vocab": z * 8 + lax.rem(x + d, 4) * 2 + yl}
 
+    zy = z * 2 + yl
+
+    def vocab_of(e):
+        return {"vocab": lax.div(e, 2) * 8 + x * 2 + lax.rem(e, 2)}
+
+    def at_zy(d):
+        return vocab_of(lax.rem(zy + d, 16))
+
     at_y = {"vocab": z * 8 + x * 2 + (1 - yl)}
 
     barrier = pltpu.get_barrier_semaphore()
-    for d in range(1, 8):
-        pl.semaphore_signal(barrier, inc=1, device_id=at_z(d), device_id_type=MESH)
+    for d in range(1, 16):
+        pl.semaphore_signal(barrier, inc=1, device_id=at_zy(d), device_id_type=MESH)
     for d in range(1, 4):
         pl.semaphore_signal(barrier, inc=1, device_id=at_x(d), device_id_type=MESH)
-    pl.semaphore_signal(barrier, inc=1, device_id=at_y, device_id_type=MESH)
     for d in range(1, 8):
         o = lax.rem(b + d, 8)
         pl.semaphore_signal(
             barrier, inc=1, device_id={"section": lax.div(o, 4), "tok": lax.rem(o, 4)}, device_id_type=MESH
         )
-    ga[z, x, yl] = rows_ref[...]
-    pl.semaphore_wait(barrier, 18)
-
-    def gather(g, ss, rs):
+    own_t = rows_ref[0].astype(F32)
+    ga[z, x, yl] = jnp.concatenate([own_t, jnp.zeros((CP - C, T), F32)], axis=0).astype(BF)
+    pl.semaphore_wait(barrier, 25)
+
+    def gather_y(g, ss, rs):
         rcopy(g.at[z, x, yl], g.at[z, x, yl], ss.at[0], rs.at[0], at_y)
         await_bytes(g.at[z, x, 1 - yl], rs.at[0])
+
+    def gather(g, ss, rs):
         for d in (4, 3, 5, 2, 6, 1, 7):
             rcopy(g.at[z, x], g.at[z, x], ss.at[1], rs.at[1], at_z(d))
         await_bytes(g.at[pl.ds(0, 7), x], rs.at[1])
@@ -147,6 +160,7 @@
 
     pcopy = pltpu.make_async_copy(proj_ref, proj, loc_sem.at[0])
     pcopy.start()
+    gather_y(ga, g1s, g1r)
     ring_start(w_own, w_piece, w_s, w_r)
     wcopy = pltpu.make_async_copy(w_ref, wf.at[pl.ds(pl.multiple_of(KB * b, 64), KB), :], loc_sem.at[1])
     wcopy.start()
@@ -175,10 +189,7 @@
     gather(ga, g1s, g1r)
     inv1 = normalize(ga)
     pcopy.wait()
-    part = lax.dot_general(
-        proj[pl.ds(pl.multiple_of(s * D, D), D), :], rt[...], (((0,), (0,)), ((), ())),
-        preferred_element_type=F32,
-    )
+    part = jnp.dot(proj[:, pl.ds(pl.multiple_of(s * D, D), D)], rt[...], preferred_element_type=F32)
     own_rows = pl.ds(pl.multiple_of(v * C, 8), C)
 
     @pl.when(s == 0)
@@ -188,7 +199,7 @@
         xch[pl.ds(CP, C), :] = normed[own_rows, :]
         xch[pl.ds(CP + C, 8), :] = jnp.zeros((8, T), F32)
         rcopy(xch, xin, x_s.at[0], x_r.at[0], sib)
-        sy[2] = jnp.broadcast_to(inv1, (8, T))
+        inv_keep[...] = jnp.broadcast_to(inv1, (8, T))
         ring_mid(w_piece, w_s, w_r)
 
     @pl.when(s == 1)
@@ -196,9 +207,19 @@
         await_bytes(xin, x_r.at[0])
         mixed = part + xin[pl.ds(0, C), :]
         gb[z, x, yl] = jnp.concatenate([mixed, jnp.zeros((CP - C, T), F32)], axis=0).astype(BF)
+        gather_y(gb, g2s, g2r)
         gather(gb, g2s, g2r)
-        sy[2] = jnp.broadcast_to(normalize(gb), (8, T))
+        inv_keep[...] = jnp.broadcast_to(normalize(gb), (8, T))
         ring_mid(w_piece, w_s, w_r)
+
+    @pl.when(s == 1)
+    def _():
+        def turn_proj(i, carry):
+            r = pl.multiple_of(i * T, T)
+            ph[pl.ds(r, T), :] = proj[:, pl.ds(r, T)].astype(F32).T.astype(BF)
+            return carry
+
+        lax.fori_loop(0, D // T, turn_proj, 0)
 
     def turn(i, carry):
         r = pl.multiple_of(i * T, T)
@@ -228,7 +249,7 @@
     lax.fori_loop(0, 4, logits_tile, 0)
     r_all[:, pl.ds(pl.multiple_of(b * T, T), T)] = rt[pl.ds(pl.multiple_of(b * KB, 64), KB), :]
 
-    label = lab_ref[...]
+    label = lab_ref[...] - v * VS
     place = lax.broadcasted_iota(jnp.int32, (VS, T), 0)
     hit = place == label
     values = logt[...]
@@ -256,14 +277,11 @@
     for d in (2, 1, 3):
         rcopy(sx.at[x], sx.at[x], st_s.at[0], st_r.at[0], at_x(d))
     await_bytes(sx.at[pl.ds(0, 3)], st_r.at[0])
-    sz[z] = combine([sx[i] for i in range(4)])
-    for d in (4, 3, 5, 2, 6, 1, 7):
-        rcopy(sz.at[z], sz.at[z], st_s.at[1], st_r.at[1], at_z(d))
-    await_bytes(sz.at[pl.ds(0, 7)], st_r.at[1])
-    sy[yl] = combine([sz[i] for i in range(8)])
-    rcopy(sy.at[yl], sy.at[yl], st_s.at[2], st_r.at[2], at_y)
-    await_bytes(sy.at[1 - yl], st_r.at[2])
-    stats = combine([sy[0], sy[1]])
+    sz[zy] = combine([sx[i] for i in range(4)])
+    for d in ORDER:
+        rcopy(sz.at[zy], sz.at[zy], st_s.at[1], st_r.at[1], at_zy(d))
+    await_bytes(sz.at[pl.ds(0, 15)], st_r.at[1])
+    stats = combine([sz[i] for i in range(16)])
     weighting = jnp.where(s == 1, MTP_WEIGHT, 1.0).astype(F32)
     inv_den = 1.0 / stats[1:2]
     mean_dot = weighting * (stats[2:3] * inv_den - stats[3:4]) * (1.0 / D)
@@ -278,56 +296,56 @@
         for j in range(8):
             p[i, j // 2, j % 2] = jnp.concatenate([block[C * j:C * (j + 1), :], pad], axis=0).astype(BF)
 
-    def feature(i, carry):
-        r = pl.multiple_of(i * KB, KB)
-        block = jnp.dot(wf[pl.ds(r, KB), :], lgt, preferred_element_type=F32)
-        spread(block, p3, i)
-        return carry
-
-    lax.fori_loop(0, 8, feature, 0)
-
-    def scatter(p, rx, az, af, rz, by, ry, ss, rs):
-        for d in (2, 1, 3):
-            xo = lax.rem(x + d, 4)
-            rcopy(p.at[:, xo], rx.at[x], ss.at[0], rs.at[0], at_x(d))
-
-        def rest():
-            await_bytes(rx.at[pl.ds(0, 3)], rs.at[0])
-
-            def add(i, carry):
+    def group(d):
+        return lax.rem(lax.div(z, GROUP) + d, GROUPS)
+
+    def blocks(d):
+        return pl.ds(pl.multiple_of(group(d) * GROUP, GROUP), GROUP)
+
+    def scatter_x(make, p, rx, ss, rs):
+        for n in range(GROUPS):
+            d = GROUPS - 1 - n
+            for k in range(GROUP):
+                make(group(d) * GROUP + k)
+            for dx in (2, 1, 3):
+                xo = lax.rem(x + dx, 4)
+                rcopy(p.at[blocks(d), xo], rx.at[x, blocks(d)], ss, rs.at[d], at_x(dx))
+
+    def scatter_zy(p, rx, az, af, rz, ss, rs, ss2, rs2):
+        for n in range(GROUPS):
+            d = GROUPS - 1 - n
+            await_bytes(rx.at[pl.ds(0, 3), blocks(d)], rs.at[d])
+            for k in range(GROUP):
+                i = group(d) * GROUP + k
                 for j in range(2):
                     a = p[i, x, j].astype(F32)
-                    for d in range(1, 4):
-                        a = a + rx[lax.rem(x + d, 4), i, j].astype(F32)
-                    af[i, j] = a
-                    az[i, j] = a.astype(BF)
-                return carry
-
-            lax.fori_loop(0, 8, add, 0)
-            for d in (4, 3, 5, 2, 6, 1, 7):
-                zo = lax.rem(z + d, 8)
-                rcopy(az.at[zo], rz.at[z], ss.at[1], rs.at[1], at_z(d))
-            await_bytes(rz.at[pl.ds(0, 7)], rs.at[1])
-            for j in range(2):
-                a = af[z, j]
-                for d in range(1, 8):
-                    a = a + rz[lax.rem(z + d, 8), j].astype(F32)
-                by[j] = a
-            rcopy(by.at[1 - yl], ry, ss.at[2], rs.at[2], at_y)
-            await_bytes(ry, rs.at[2])
-            return (by[yl] + ry[...])[:C, :]
-
-        return rest
-
-    def scatter_sent(rx, rz, ry, ss):
-        await_bytes(rx.at[pl.ds(0, 3)], ss.at[0])
-        await_bytes(rz.at[pl.ds(0, 7)], ss.at[1])
-        await_bytes(ry, ss.at[2])
-
-    rest = scatter(p3, rx3, az3, af3, rz3, by3, ry3, q3s, q3r)
+                    for dx in range(1, 4):
+                        a = a + rx[lax.rem(x + dx, 4), i, j].astype(F32)
+                    e = i * 2 + j
+                    af[e] = a
+                    az[e] = a.astype(BF)
+
+                    @pl.when(e != zy)
+                    def _():
+                        rcopy(az.at[e], rz.at[zy], ss2, rs2, vocab_of(e))
+        await_bytes(rz.at[pl.ds(0, 15)], rs2)
+        a = af[zy]
+        for d in range(1, 16):
+            a = a + rz[lax.rem(zy + d, 16)].astype(F32)
+        return a[:C, :]
+
+    def scatter_sent(rx, rz, ss, ss2):
+        await_bytes(rx.at[pl.ds(0, 3)], ss)
+        await_bytes(rz.at[pl.ds(0, 15)], ss2)
+
+    def feature(i):
+        block = jnp.dot(wf[pl.ds(pl.multiple_of(i * KB, KB), KB), :], lgt, preferred_element_type=F32)
+        spread(block, p3, i)
+
+    scatter_x(feature, p3, rx3, q3s.at[0], q3r)
     lax.fori_loop(1, 8, to_owner, 0)
-    fgrad = rest()
-    back = (fgrad - normed[own_rows, :] * mean_dot) * sy[2][0:1]
+    fgrad = scatter_zy(p3, rx3, az3, af3, rz3, q3s.at[0], q3r, q3s.at[1], q3r.at[8])
+    back = (fgrad - normed[own_rows, :] * mean_dot) * inv_keep[0:1]
 
     def head_grad():
         await_bytes(r_all.at[:, pl.ds(0, 7 * T)], r_r)
@@ -358,32 +376,26 @@
     def _():
         mg = back.astype(BF)
 
-        def joined(i, carry):
-            r = pl.multiple_of(i * KB, KB)
-            block = jnp.dot(proj[pl.ds(r, KB), :], mg, preferred_element_type=F32)
+        def joined(i):
+            block = jnp.dot(ph[pl.ds(pl.multiple_of(i * KB, KB), KB), :], mg, preferred_element_type=F32)
             spread(block, p4, i)
-            return carry
-
-        lax.fori_loop(0, 8, joined, 0)
-        rest4 = scatter(p4, rx4, az4, af4, rz4, by4, ry4, q4s, q4r)
+
+        scatter_x(joined, p4, rx4, q4s.at[0], q4r)
         hdot = jnp.sum(mg.astype(F32) * xin[pl.ds(0, C), :], axis=0, keepdims=True)
         hx[x] = jnp.broadcast_to(hdot, (8, T))
         for d in (2, 1, 3):
             rcopy(hx.at[x], hx.at[x], h_s.at[0], h_r.at[0], at_x(d))
         ring_mid(l_piece, l_s, l_r)
         await_bytes(hx.at[pl.ds(0, 3)], h_r.at[0])
-        hz[z] = hx[0] + hx[1] + hx[2] + hx[3]
-        for d in (4, 3, 5, 2, 6, 1, 7):
-            rcopy(hz.at[z], hz.at[z], h_s.at[1], h_r.at[1], at_z(d))
-        jgrad = rest4()
-        await_bytes(hz.at[pl.ds(0, 7)], h_r.at[1])
+        hz[zy] = hx[0] + hx[1] + hx[2] + hx[3]
+        for d in ORDER:
+            rcopy(hz.at[zy], hz.at[zy], h_s.at[1], h_r.at[1], at_zy(d))
+        jgrad = scatter_zy(p4, rx4, az4, af4, rz4, q4s.at[0], q4r, q4s.at[1], q4r.at[8])
+        await_bytes(hz.at[pl.ds(0, 15)], h_r.at[1])
         tot = hz[0]
-        for i in range(1, 8):
+        for i in range(1, 16):
             tot = tot + hz[i]
-        hy[yl] = tot
-        rcopy(hy.at[yl], hy.at[yl], h_s.at[2], h_r.at[2], at_y)
-        await_bytes(hy.at[1 - yl], h_r.at[2])
-        hmean = (hy[0] + hy[1])[0:1] * (1.0 / D)
+        hmean = tot[0:1] * (1.0 / D)
         depth = (jgrad - xin[pl.ds(CP, C), :] * hmean) * xin[pl.ds(C, 1), :]
         bk[...] = depth
         rcopy(bk, bkin, x_s.at[1], x_r.at[1], sib)
@@ -391,25 +403,21 @@
         out_ref[...] = bkin[...] + depth
         head_grad()
         gather_sent(gb, g2s)
-        scatter_sent(rx4, rz4, ry4, q4s)
+        scatter_sent(rx4, rz4, q4s.at[0], q4s.at[1])
         await_bytes(hx.at[pl.ds(0, 3)], h_s.at[0])
-        await_bytes(hz.at[pl.ds(0, 7)], h_s.at[1])
-        await_bytes(hy.at[0], h_s.at[2])
+        await_bytes(hz.at[pl.ds(0, 15)], h_s.at[1])
 
     await_bytes(bk, x_s.at[1])
     gather_sent(ga, g1s)
-    scatter_sent(rx3, rz3, ry3, q3s)
+    scatter_sent(rx3, rz3, q3s.at[0], q3s.at[1])
     await_bytes(sx.at[pl.ds(0, 3)], st_s.at[0])
-    await_bytes(sz.at[pl.ds(0, 7)], st_s.at[1])
-    await_bytes(sy.at[0], st_s.at[2])
+    await_bytes(sz.at[pl.ds(0, 15)], st_s.at[1])
     await_bytes(r_all.at[:, pl.ds(0, 7 * T)], r_s)
     await_bytes(wf.at[pl.ds(0, 7 * KB), :], w_s)
     await_bytes(lg_all.at[:, pl.ds(0, 7 * T)], l_s)
 
 
 def local(rows, targets, proj_weight, head_weight):
-    rows_t = jnp.pad(rows[0].T, ((0, CP - C), (0, 0)))
-    labels = targets - lax.axis_index("vocab") * VS
     vm = pl.BlockSpec(memory_space=pltpu.VMEM)
     anyspace = pl.BlockSpec(memory_space=pl.ANY)
     dma = pltpu.SemaphoreType.DMA
@@ -418,11 +426,9 @@
         return [
             pltpu.VMEM((8, 4, 2, CP, T), BF),
             pltpu.VMEM((4, 8, 2, CP, T), BF),
-            pltpu.VMEM((8, 2, CP, T), BF),
-            pltpu.VMEM((8, 2, CP, T), F32),
-            pltpu.VMEM((8, 2, CP, T), BF),
-            pltpu.VMEM((2, CP, T), F32),
-            pltpu.VMEM((CP, T), F32),
+            pltpu.VMEM((16, CP, T), BF),
+            pltpu.VMEM((16, CP, T), F32),
+            pltpu.VMEM((16, CP, T), BF),
         ]
 
     head_grad, grad_t = pl.pallas_call(
@@ -435,7 +441,8 @@
         out_specs=(vm, vm),
         scratch_shapes=[
             pltpu.VMEM((D, VS), BF),
-            pltpu.VMEM((2 * D, C), BF),
+            pltpu.VMEM((C, 2 * D), BF),
+            pltpu.VMEM((D, C), BF),
             pltpu.VMEM((8, 4, 2, CP, T), BF),
             pltpu.VMEM((8, 4, 2, CP, T), BF),
             pltpu.VMEM((D, T), F32),
@@ -447,19 +454,18 @@
             *rs_bufs(),
             *rs_bufs(),
             pltpu.VMEM((4, 8, T), F32),
-            pltpu.VMEM((8, 8, T), F32),
-            pltpu.VMEM((3, 8, T), F32),
+            pltpu.VMEM((16, 8, T), F32),
+            pltpu.VMEM((8, T), F32),
             pltpu.VMEM((4, 8, T), F32),
-            pltpu.VMEM((8, 8, T), F32),
-            pltpu.VMEM((2, 8, T), F32),
+            pltpu.VMEM((16, 8, T), F32),
             pltpu.VMEM((2 * CP, T), F32),
             pltpu.VMEM((2 * CP, T), F32),
             pltpu.VMEM((C, T), F32),
             pltpu.VMEM((C, T), F32),
             dma((2,)), dma, dma((7,)), dma, dma((7,)), dma, dma,
             dma((3,)), dma((6,)), dma((3,)), dma((6,)),
-            dma((3,)), dma((3,)), dma((3,)), dma((3,)),
-            dma((3,)), dma((3,)), dma((3,)), dma((3,)),
+            dma((2,)), dma((2,)), dma((2,)), dma((2,)),
+            dma((2,)), dma((9,)), dma((2,)), dma((9,)),
             dma((2,)), dma((2,)),
         ],
         compiler_params=pltpu.CompilerParams(
@@ -467,7 +473,7 @@
         ),
         cost_estimate=pl.CostEstimate(flops=3 * 10**9, bytes_accessed=2 * 10**7, transcendentals=3 * 10**5),
         name="head",
-    )(rows_t, labels, proj_weight, head_weight)
+    )(jnp.swapaxes(rows, 1, 2), targets, proj_weight.T, head_weight)
     return head_grad, grad_t.T
 
 

time: 184 us -> 148 us (0.80)
  Pallas kernels: 175 us -> 144 us
  local copies, waits for them, and re-layouts: 6.69 us -> 2.78 us
    pallas_call x1, Pallas kernels: 175 us -> 144 us  [local(): pl.pallas_call(kernel, out_shape=(jax.ShapeDtypeStruct((KB, VS), BF), jax...]
    unnamed x5 -> x4, local copies, waits for them, and re-layouts: 5.37 us -> 2.78 us
where the time goes in v2:
time: 148 us
  Pallas kernels  144 us (97%)
  local copies, waits for them, and re-layouts  2.78 us (2%)
    pallas_call x1, Pallas kernels, local(): pl.pallas_call(kernel, out_shape=(jax.ShapeDtypeStruct((KB, VS), BF), jax...  144 us

profile of v2, /device:TPU:48, one launch (start us, length us, event | category | flops | bytes accessed | tf_op | source)
XLA Modules:
  0.0 147.9 jit_solution(5120225480529303097)
XLA Ops:
  0.6 144.4 %head.1 = (bf16[448,1024]{1,0:T(8,128)(2,1)}, f32[56,128]{1,0:T(8,128)}) custom-call(bf16[1,56,128]{2,1,0:T(8,128)(2,1)} %bitcast.5, s32[1,128]{1,0:T(1,128)} %lab_ref.1, bf16[56,7168]{1,0:T(8,128)(2,1)} %bitcast.4, bf16[448,1024]{1,0:T(8,128)(2,1)} %w_ref.1), custom_call_target="tpu_custom_call" | custom-call | flops 3000000000 | bytes 20000000 | tf_op jit(solution)/shard_map/head/pallas_call | solution.py:434
  145.1 0.0 copy-start
  145.1 2.2 %copy.8 = bf16[448,1024]{1,0:T(8,128)(2,1)} copy(bf16[448,1024]{1,0:T(8,128)(2,1)} %get-tuple-element.8) | data formatting | bytes 1835008
  147.3 0.0 copy-done
  147.3 0.6 copy.9
Async XLA Ops:
  145.1 2.2 %copy-start = (f32[56,128]{1,0:T(8,128)S(1)}, f32[56,128]{1,0:T(8,128)}, u32[]{:S(2)}) copy-start(f32[56,128]{1,0:T(8,128)} %get-tuple-element.5) | copy-start | bytes 86020

commit v3 on v2

--- a/solution.py
+++ b/solution.py
@@ -36,11 +36,10 @@
     rows_ref, lab_ref, proj_ref, w_ref, hg_ref, out_ref,
     wf, proj, ph, ga, gb, normed, rt, rnd, logt, lg_all, r_all,
     p3, rx3, az3, af3, rz3,
-    p4, rx4, az4, af4, rz4,
-    sx, sz, inv_keep, hx, hz,
+    phr, pb, mgb, jb, jx, sx, sz, inv_keep,
     xch, xin, bk, bkin,
     loc_sem, w_s, w_r, l_s, l_r, r_s, r_r,
-    g1s, g1r, g2s, g2r, st_s, st_r, h_s, h_r, q3s, q3r, q4s, q4r, x_s, x_r,
+    g1s, g1r, g2s, g2r, st_s, st_r, q3s, q3r, p_s, p_r, m_s, m_r, j_s, j_r, x_s, x_r,
 ):
     s = lax.axis_index("section")
     v = lax.axis_index("vocab")
@@ -68,13 +67,18 @@
     def at_zy(d):
         return vocab_of(lax.rem(zy + d, 16))
 
+    xy = x * 2 + yl
+
+    def at_xy(d):
+        return {"vocab": z * 8 + lax.rem(xy + d, 8)}
+
     at_y = {"vocab": z * 8 + x * 2 + (1 - yl)}
 
     barrier = pltpu.get_barrier_semaphore()
     for d in range(1, 16):
         pl.semaphore_signal(barrier, inc=1, device_id=at_zy(d), device_id_type=MESH)
-    for d in range(1, 4):
-        pl.semaphore_signal(barrier, inc=1, device_id=at_x(d), device_id_type=MESH)
+    for d in range(1, 8):
+        pl.semaphore_signal(barrier, inc=1, device_id=at_xy(d), device_id_type=MESH)
     for d in range(1, 8):
         o = lax.rem(b + d, 8)
         pl.semaphore_signal(
@@ -82,7 +86,7 @@
         )
     own_t = rows_ref[0].astype(F32)
     ga[z, x, yl] = jnp.concatenate([own_t, jnp.zeros((CP - C, T), F32)], axis=0).astype(BF)
-    pl.semaphore_wait(barrier, 25)
+    pl.semaphore_wait(barrier, 29)
 
     def gather_y(g, ss, rs):
         rcopy(g.at[z, x, yl], g.at[z, x, yl], ss.at[0], rs.at[0], at_y)
@@ -186,9 +190,28 @@
         lax.fori_loop(0, 8, scale, 0)
         return inv
 
+    pcopy.wait()
+
+    @pl.when(s == 1)
+    def _():
+        odd = lax.rem(z, 2) == 1
+
+        def turn_proj(i, carry):
+            r = pl.multiple_of(i * T, T)
+            block = proj[:, pl.ds(r, T)].astype(F32)
+            even_place = jnp.concatenate([block, jnp.zeros((T - C, T), F32)], axis=0)
+            odd_place = jnp.concatenate([jnp.zeros((CP, T), F32), block, jnp.zeros((CP - C, T), F32)], axis=0)
+            ph[pl.ds(r, T), :] = jnp.where(odd, odd_place, even_place).T.astype(BF)
+            return carry
+
+        lax.fori_loop(0, D // T, turn_proj, 0)
+        for d in (4, 3, 5, 2, 6, 1, 7):
+            zo = lax.rem(z + d, 8)
+            rcopy(ph.at[pl.ds(pl.multiple_of(zo * KB, 64), KB), :], phr.at[z], p_s, p_r, at_z(d))
+        phr[z] = ph[pl.ds(pl.multiple_of(z * KB, 64), KB), :]
+
     gather(ga, g1s, g1r)
     inv1 = normalize(ga)
-    pcopy.wait()
     part = jnp.dot(proj[:, pl.ds(pl.multiple_of(s * D, D), D)], rt[...], preferred_element_type=F32)
     own_rows = pl.ds(pl.multiple_of(v * C, 8), C)
 
@@ -211,15 +234,9 @@
         gather(gb, g2s, g2r)
         inv_keep[...] = jnp.broadcast_to(normalize(gb), (8, T))
         ring_mid(w_piece, w_s, w_r)
-
-    @pl.when(s == 1)
-    def _():
-        def turn_proj(i, carry):
-            r = pl.multiple_of(i * T, T)
-            ph[pl.ds(r, T), :] = proj[:, pl.ds(r, T)].astype(F32).T.astype(BF)
-            return carry
-
-        lax.fori_loop(0, D // T, turn_proj, 0)
+        await_bytes(phr.at[pl.ds(0, 7)], p_r)
+        for i in range(4):
+            pb[:, pl.ds(i * T, T)] = phr[2 * i] + phr[2 * i + 1]
 
     def turn(i, carry):
         r = pl.multiple_of(i * T, T)
@@ -273,22 +290,22 @@
             l_ = l_ + q[3:4]
         return jnp.concatenate([m, d_, e_, l_, jnp.zeros((4, T), F32)], axis=0)
 
-    sx[x] = jnp.concatenate([top, den, sel, lab, jnp.zeros((4, T), F32)], axis=0)
-    for d in (2, 1, 3):
-        rcopy(sx.at[x], sx.at[x], st_s.at[0], st_r.at[0], at_x(d))
-    await_bytes(sx.at[pl.ds(0, 3)], st_r.at[0])
-    sz[zy] = combine([sx[i] for i in range(4)])
-    for d in ORDER:
-        rcopy(sz.at[zy], sz.at[zy], st_s.at[1], st_r.at[1], at_zy(d))
-    await_bytes(sz.at[pl.ds(0, 15)], st_r.at[1])
-    stats = combine([sz[i] for i in range(16)])
+    sx[xy] = jnp.concatenate([top, den, sel, lab, jnp.zeros((4, T), F32)], axis=0)
+    for d in (4, 5, 3, 1, 7, 2, 6):
+        rcopy(sx.at[xy], sx.at[xy], st_s.at[0], st_r.at[0], at_xy(d))
+    lax.fori_loop(1, 8, to_owner, 0)
+    await_bytes(sx.at[pl.ds(0, 7)], st_r.at[0])
+    sz[z] = combine([sx[i] for i in range(8)])
+    for d in (4, 3, 5, 2, 6, 1, 7):
+        rcopy(sz.at[z], sz.at[z], st_s.at[1], st_r.at[1], at_z(d))
+    await_bytes(sz.at[pl.ds(0, 7)], st_r.at[1])
+    stats = combine([sz[i] for i in range(8)])
     weighting = jnp.where(s == 1, MTP_WEIGHT, 1.0).astype(F32)
     inv_den = 1.0 / stats[1:2]
     mean_dot = weighting * (stats[2:3] * inv_den - stats[3:4]) * (1.0 / D)
     prob = jnp.exp(logt[...] - stats[0:1]) * inv_den
     lgt = (weighting * (prob - hit.astype(F32))).astype(BF)
     lg_all[:, pl.ds(pl.multiple_of(b * T, T), T)] = lgt
-    ring_start(l_own, l_piece, l_s, l_r)
 
     pad = jnp.zeros((CP - C, T), F32)
 
@@ -328,6 +345,7 @@
                     @pl.when(e != zy)
                     def _():
                         rcopy(az.at[e], rz.at[zy], ss2, rs2, vocab_of(e))
+        ring_start(l_own, l_piece, l_s, l_r)
         await_bytes(rz.at[pl.ds(0, 15)], rs2)
         a = af[zy]
         for d in range(1, 16):
@@ -343,7 +361,6 @@
         spread(block, p3, i)
 
     scatter_x(feature, p3, rx3, q3s.at[0], q3r)
-    lax.fori_loop(1, 8, to_owner, 0)
     fgrad = scatter_zy(p3, rx3, az3, af3, rz3, q3s.at[0], q3r, q3s.at[1], q3r.at[8])
     back = (fgrad - normed[own_rows, :] * mean_dot) * inv_keep[0:1]
 
@@ -375,27 +392,32 @@
     @pl.when(s == 1)
     def _():
         mg = back.astype(BF)
-
-        def joined(i):
-            block = jnp.dot(ph[pl.ds(pl.multiple_of(i * KB, KB), KB), :], mg, preferred_element_type=F32)
-            spread(block, p4, i)
-
-        scatter_x(joined, p4, rx4, q4s.at[0], q4r)
         hdot = jnp.sum(mg.astype(F32) * xin[pl.ds(0, C), :], axis=0, keepdims=True)
-        hx[x] = jnp.broadcast_to(hdot, (8, T))
-        for d in (2, 1, 3):
-            rcopy(hx.at[x], hx.at[x], h_s.at[0], h_r.at[0], at_x(d))
+        high = hdot.astype(BF).astype(F32)
+        middle = (hdot - high).astype(BF).astype(F32)
+        low = hdot - high - middle
+        mgb[z] = jnp.concatenate(
+            [mg.astype(F32), high, middle, low, jnp.zeros((5, T), F32)], axis=0
+        ).astype(BF)
+        for d in (4, 3, 5, 2, 6, 1, 7):
+            rcopy(mgb.at[z], mgb.at[z], m_s, m_r, at_z(d))
+        await_bytes(mgb.at[pl.ds(0, 7)], m_r)
+        hsum = jnp.zeros((8, T), F32)
+        for i in range(8):
+            hsum = hsum + mgb[i, pl.ds(C - 8, 16), :].astype(F32)[8:16]
+        hrow = hsum[0:1] + hsum[1:2] + hsum[2:3]
+        joint = jnp.dot(pb[...], mgb[...].reshape(8 * CP, T), preferred_element_type=F32)
+        for j in range(8):
+            jb[j] = jnp.concatenate([joint[C * j:C * (j + 1), :], jnp.broadcast_to(hrow, (8, T))], axis=0)
+        for d in (4, 5, 3, 1, 7, 2, 6):
+            rcopy(jb.at[lax.rem(xy + d, 8)], jx.at[xy], j_s, j_r, at_xy(d))
         ring_mid(l_piece, l_s, l_r)
-        await_bytes(hx.at[pl.ds(0, 3)], h_r.at[0])
-        hz[zy] = hx[0] + hx[1] + hx[2] + hx[3]
-        for d in ORDER:
-            rcopy(hz.at[zy], hz.at[zy], h_s.at[1], h_r.at[1], at_zy(d))
-        jgrad = scatter_zy(p4, rx4, az4, af4, rz4, q4s.at[0], q4r, q4s.at[1], q4r.at[8])
-        await_bytes(hz.at[pl.ds(0, 15)], h_r.at[1])
-        tot = hz[0]
-        for i in range(1, 16):
-            tot = tot + hz[i]
-        hmean = tot[0:1] * (1.0 / D)
+        await_bytes(jx.at[pl.ds(0, 7)], j_r)
+        tot = jb[xy]
+        for d in range(1, 8):
+            tot = tot + jx[lax.rem(xy + d, 8)]
+        jgrad = tot[:C, :]
+        hmean = tot[C:C + 1] * (1.0 / D)
         depth = (jgrad - xin[pl.ds(CP, C), :] * hmean) * xin[pl.ds(C, 1), :]
         bk[...] = depth
         rcopy(bk, bkin, x_s.at[1], x_r.at[1], sib)
@@ -403,15 +425,15 @@
         out_ref[...] = bkin[...] + depth
         head_grad()
         gather_sent(gb, g2s)
-        scatter_sent(rx4, rz4, q4s.at[0], q4s.at[1])
-        await_bytes(hx.at[pl.ds(0, 3)], h_s.at[0])
-        await_bytes(hz.at[pl.ds(0, 15)], h_s.at[1])
+        await_bytes(mgb.at[pl.ds(0, 7)], m_s)
+        await_bytes(jx.at[pl.ds(0, 7)], j_s)
+        await_bytes(phr.at[pl.ds(0, 7)], p_s)
 
     await_bytes(bk, x_s.at[1])
     gather_sent(ga, g1s)
     scatter_sent(rx3, rz3, q3s.at[0], q3s.at[1])
-    await_bytes(sx.at[pl.ds(0, 3)], st_s.at[0])
-    await_bytes(sz.at[pl.ds(0, 15)], st_s.at[1])
+    await_bytes(sx.at[pl.ds(0, 7)], st_s.at[0])
+    await_bytes(sz.at[pl.ds(0, 7)], st_s.at[1])
     await_bytes(r_all.at[:, pl.ds(0, 7 * T)], r_s)
     await_bytes(wf.at[pl.ds(0, 7 * KB), :], w_s)
     await_bytes(lg_all.at[:, pl.ds(0, 7 * T)], l_s)
@@ -442,7 +464,7 @@
         scratch_shapes=[
             pltpu.VMEM((D, VS), BF),
             pltpu.VMEM((C, 2 * D), BF),
-            pltpu.VMEM((D, C), BF),
+            pltpu.VMEM((D, T), BF),
             pltpu.VMEM((8, 4, 2, CP, T), BF),
             pltpu.VMEM((8, 4, 2, CP, T), BF),
             pltpu.VMEM((D, T), F32),
@@ -452,20 +474,22 @@
             pltpu.VMEM((VS, 8 * T), BF),
             pltpu.VMEM((KB, 8 * T), BF),
             *rs_bufs(),
-            *rs_bufs(),
-            pltpu.VMEM((4, 8, T), F32),
-            pltpu.VMEM((16, 8, T), F32),
+            pltpu.VMEM((8, KB, T), BF),
+            pltpu.VMEM((KB, 8 * CP), BF),
+            pltpu.VMEM((8, CP, T), BF),
+            pltpu.VMEM((8, CP, T), F32),
+            pltpu.VMEM((8, CP, T), F32),
+            pltpu.VMEM((8, 8, T), F32),
+            pltpu.VMEM((8, 8, T), F32),
             pltpu.VMEM((8, T), F32),
-            pltpu.VMEM((4, 8, T), F32),
-            pltpu.VMEM((16, 8, T), F32),
             pltpu.VMEM((2 * CP, T), F32),
             pltpu.VMEM((2 * CP, T), F32),
             pltpu.VMEM((C, T), F32),
             pltpu.VMEM((C, T), F32),
             dma((2,)), dma, dma((7,)), dma, dma((7,)), dma, dma,
             dma((3,)), dma((6,)), dma((3,)), dma((6,)),
-            dma((2,)), dma((2,)), dma((2,)), dma((2,)),
-            dma((2,)), dma((9,)), dma((2,)), dma((9,)),
+            dma((2,)), dma((2,)), dma((2,)), dma((9,)),
+            dma, dma, dma, dma, dma, dma,
             dma((2,)), dma((2,)),
         ],
         compiler_params=pltpu.CompilerParams(

time: 148 us -> 150 us (1.014)
  the two profiles are of different devices: /device:TPU:48 before, /device:TPU:1 now
where the time goes in v3:
time: 150 us
  Pallas kernels  147 us (98%)
  local copies, waits for them, and re-layouts  2.78 us (2%)
    pallas_call x1, Pallas kernels, local(): pl.pallas_call(kernel, out_shape=(jax.ShapeDtypeStruct((KB, VS), BF), jax...  147 us

profile of v3, /device:TPU:1, one launch (start us, length us, event | category | flops | bytes accessed | tf_op | source)
XLA Modules:
  0.0 150.0 jit_solution(7430959405358186387)
XLA Ops:
  0.6 146.6 %head.1 = (bf16[448,1024]{1,0:T(8,128)(2,1)}, f32[56,128]{1,0:T(8,128)}) custom-call(bf16[1,56,128]{2,1,0:T(8,128)(2,1)} %bitcast.5, s32[1,128]{1,0:T(1,128)} %lab_ref.1, bf16[56,7168]{1,0:T(8,128)(2,1)} %bitcast.4, bf16[448,1024]{1,0:T(8,128)(2,1)} %w_ref.1), custom_call_target="tpu_custom_call" | custom-call | flops 3000000000 | bytes 20000000 | tf_op jit(solution)/shard_map/head/pallas_call | solution.py:456
  147.2 0.0 copy-start
  147.2 2.2 %copy.8 = bf16[448,1024]{1,0:T(8,128)(2,1)} copy(bf16[448,1024]{1,0:T(8,128)(2,1)} %get-tuple-element.8) | data formatting | bytes 1835008
  149.4 0.0 copy-done
  149.4 0.6 copy.9
Async XLA Ops:
  147.2 2.2 %copy-start = (f32[56,128]{1,0:T(8,128)S(1)}, f32[56,128]{1,0:T(8,128)}, u32[]{:S(2)}) copy-start(f32[56,128]{1,0:T(8,128)} %get-tuple-element.5) | copy-start | bytes 86020

commit v4 on v3

--- a/solution.py
+++ b/solution.py
@@ -13,6 +13,7 @@
 CP = 64
 VS = 1024
 KB = 448
+SHARE = KB // 4
 MESH = pl.DeviceIdType.MESH
 ORDER = (8, 7, 9, 6, 10, 5, 11, 4, 12, 3, 13, 2, 14, 1, 15)
 GROUP = 2
@@ -39,7 +40,7 @@
     phr, pb, mgb, jb, jx, sx, sz, inv_keep,
     xch, xin, bk, bkin,
     loc_sem, w_s, w_r, l_s, l_r, r_s, r_r,
-    g1s, g1r, g2s, g2r, st_s, st_r, q3s, q3r, p_s, p_r, m_s, m_r, j_s, j_r, x_s, x_r,
+    g1s, g1r, g2s, g2r, st_s, st_r, q3s, q3r, p_s, p_r, m_s, m_r, j_s, j_r, ra_s, ra_r, x_s, x_r,
 ):
     s = lax.axis_index("section")
     v = lax.axis_index("vocab")
@@ -119,6 +120,10 @@
         left = {"tok": t_left}
         rcopy(own(0), piece(b, 0), ss, rs.at[0], right)
         rcopy(own(1), piece(b, 1), ss, rs.at[3], left)
+
+    def ring_second(own, piece, ss, rs):
+        right = {"tok": t_right}
+        left = {"tok": t_left}
         rcopy(own(0), piece(b, 0), ss, rs.at[6], sib)
         rcopy(own(1), piece(b, 1), ss, rs.at[6], sib)
         rcopy(own(1), piece(b, 1), ss, rs.at[1], right)
@@ -166,6 +171,7 @@
     pcopy.start()
     gather_y(ga, g1s, g1r)
     ring_start(w_own, w_piece, w_s, w_r)
+    ring_second(w_own, w_piece, w_s, w_r)
     wcopy = pltpu.make_async_copy(w_ref, wf.at[pl.ds(pl.multiple_of(KB * b, 64), KB), :], loc_sem.at[1])
     wcopy.start()
 
@@ -230,10 +236,11 @@
         await_bytes(xin, x_r.at[0])
         mixed = part + xin[pl.ds(0, C), :]
         gb[z, x, yl] = jnp.concatenate([mixed, jnp.zeros((CP - C, T), F32)], axis=0).astype(BF)
-        gather_y(gb, g2s, g2r)
+        rcopy(gb.at[z, x, yl], gb.at[z, x, yl], g2s.at[0], g2r.at[0], at_y)
+        ring_mid(w_piece, w_s, w_r)
+        await_bytes(gb.at[z, x, 1 - yl], g2r.at[0])
         gather(gb, g2s, g2r)
         inv_keep[...] = jnp.broadcast_to(normalize(gb), (8, T))
-        ring_mid(w_piece, w_s, w_r)
         await_bytes(phr.at[pl.ds(0, 7)], p_r)
         for i in range(4):
             pb[:, pl.ds(i * T, T)] = phr[2 * i] + phr[2 * i + 1]
@@ -248,14 +255,24 @@
     wcopy.wait()
     await_bytes(wf.at[pl.ds(0, 4 * KB), :], w_r.at[6])
 
+    part_rows = pl.ds(pl.multiple_of(x * SHARE, 16), SHARE)
+    own_tokens = pl.ds(pl.multiple_of(b * T, T), T)
+
+    def rows_of(o):
+        return pl.ds(pl.multiple_of(o * KB + x * SHARE, 16), SHARE)
+
     def to_owner(d, carry):
         o = lax.rem(b + d, 8)
         rcopy(
-            rt.at[pl.ds(pl.multiple_of(o * KB, 64), KB), :],
-            r_all.at[:, pl.ds(pl.multiple_of(b * T, T), T)],
+            rt.at[rows_of(o), :], r_all.at[part_rows, own_tokens],
             r_s, r_r, {"section": lax.div(o, 4), "tok": lax.rem(o, 4)},
         )
         return carry
+
+    def share_rows():
+        await_bytes(r_all.at[part_rows, pl.ds(0, 7 * T)], r_r)
+        for d in (2, 1, 3):
+            rcopy(r_all.at[part_rows, :], r_all.at[part_rows, :], ra_s, ra_r, at_x(d))
 
     def logits_tile(i, carry):
         r = pl.multiple_of(i * 256, 256)
@@ -264,7 +281,7 @@
         return carry
 
     lax.fori_loop(0, 4, logits_tile, 0)
-    r_all[:, pl.ds(pl.multiple_of(b * T, T), T)] = rt[pl.ds(pl.multiple_of(b * KB, 64), KB), :]
+    r_all[part_rows, own_tokens] = rt[rows_of(b), :]
 
     label = lab_ref[...] - v * VS
     place = lax.broadcasted_iota(jnp.int32, (VS, T), 0)
@@ -307,6 +324,7 @@
     lgt = (weighting * (prob - hit.astype(F32))).astype(BF)
     lg_all[:, pl.ds(pl.multiple_of(b * T, T), T)] = lgt
 
+    ring_start(l_own, l_piece, l_s, l_r)
     pad = jnp.zeros((CP - C, T), F32)
 
     def spread(block, p, i):
@@ -345,7 +363,9 @@
                     @pl.when(e != zy)
                     def _():
                         rcopy(az.at[e], rz.at[zy], ss2, rs2, vocab_of(e))
-        ring_start(l_own, l_piece, l_s, l_r)
+        ring_second(l_own, l_piece, l_s, l_r)
+        ring_mid(l_piece, l_s, l_r)
+        share_rows()
         await_bytes(rz.at[pl.ds(0, 15)], rs2)
         a = af[zy]
         for d in range(1, 16):
@@ -365,7 +385,7 @@
     back = (fgrad - normed[own_rows, :] * mean_dot) * inv_keep[0:1]
 
     def head_grad():
-        await_bytes(r_all.at[:, pl.ds(0, 7 * T)], r_r)
+        await_bytes(r_all.at[pl.ds(0, 3 * SHARE), :], ra_r)
         ring_late(l_piece, l_s, l_r)
         await_bytes(lg_all.at[:, pl.ds(0, 4 * T)], l_r.at[6])
 
@@ -383,7 +403,6 @@
     def _():
         bk[...] = back
         rcopy(bk, bkin, x_s.at[1], x_r.at[1], sib)
-        ring_mid(l_piece, l_s, l_r)
         head_grad()
         await_bytes(bkin, x_r.at[1])
         out_ref[...] = back + bkin[...]
@@ -411,7 +430,6 @@
             jb[j] = jnp.concatenate([joint[C * j:C * (j + 1), :], jnp.broadcast_to(hrow, (8, T))], axis=0)
         for d in (4, 5, 3, 1, 7, 2, 6):
             rcopy(jb.at[lax.rem(xy + d, 8)], jx.at[xy], j_s, j_r, at_xy(d))
-        ring_mid(l_piece, l_s, l_r)
         await_bytes(jx.at[pl.ds(0, 7)], j_r)
         tot = jb[xy]
         for d in range(1, 8):
@@ -434,7 +452,8 @@
     scatter_sent(rx3, rz3, q3s.at[0], q3s.at[1])
     await_bytes(sx.at[pl.ds(0, 7)], st_s.at[0])
     await_bytes(sz.at[pl.ds(0, 7)], st_s.at[1])
-    await_bytes(r_all.at[:, pl.ds(0, 7 * T)], r_s)
+    await_bytes(r_all.at[part_rows, pl.ds(0, 7 * T)], r_s)
+    await_bytes(r_all.at[pl.ds(0, 3 * SHARE), :], ra_s)
     await_bytes(wf.at[pl.ds(0, 7 * KB), :], w_s)
     await_bytes(lg_all.at[:, pl.ds(0, 7 * T)], l_s)
 
@@ -489,7 +508,7 @@
             dma((2,)), dma, dma((7,)), dma, dma((7,)), dma, dma,
             dma((3,)), dma((6,)), dma((3,)), dma((6,)),
             dma((2,)), dma((2,)), dma((2,)), dma((9,)),
-            dma, dma, dma, dma, dma, dma,
+            dma, dma, dma, dma, dma, dma, dma, dma,
             dma((2,)), dma((2,)),
         ],
         compiler_params=pltpu.CompilerParams(

time: 150 us -> 132 us (0.88)
  Pallas kernels: 147 us -> 128 us
    pallas_call x1, Pallas kernels: 147 us -> 128 us  [local(): pl.pallas_call(kernel, out_shape=(jax.ShapeDtypeStruct((KB, VS), BF), jax...]
where the time goes in v4:
time: 132 us
  Pallas kernels  128 us (97%)
  local copies, waits for them, and re-layouts  2.78 us (2%)
    pallas_call x1, Pallas kernels, local(): pl.pallas_call(kernel, out_shape=(jax.ShapeDtypeStruct((KB, VS), BF), jax...  128 us
    unnamed x4, local copies, waits for them, and re-layouts  2.78 us

profile of v4, /device:TPU:1, one launch (start us, length us, event | category | flops | bytes accessed | tf_op | source)
XLA Modules:
  0.0 131.7 jit_solution(1933477247709999314)
XLA Ops:
  0.6 128.3 %head.1 = (bf16[448,1024]{1,0:T(8,128)(2,1)}, f32[56,128]{1,0:T(8,128)}) custom-call(bf16[1,56,128]{2,1,0:T(8,128)(2,1)} %bitcast.5, s32[1,128]{1,0:T(1,128)} %lab_ref.1, bf16[56,7168]{1,0:T(8,128)(2,1)} %bitcast.4, bf16[448,1024]{1,0:T(8,128)(2,1)} %w_ref.1), custom_call_target="tpu_custom_call" | custom-call | flops 3000000000 | bytes 20000000 | tf_op jit(solution)/shard_map/head/pallas_call | solution.py:475
  128.9 0.0 copy-start
  128.9 2.2 %copy.8 = bf16[448,1024]{1,0:T(8,128)(2,1)} copy(bf16[448,1024]{1,0:T(8,128)(2,1)} %get-tuple-element.8) | data formatting | bytes 1835008
  131.1 0.0 copy-done
  131.1 0.6 copy.9
Async XLA Ops:
  128.9 2.2 %copy-start = (f32[56,128]{1,0:T(8,128)S(1)}, f32[56,128]{1,0:T(8,128)}, u32[]{:S(2)}) copy-start(f32[56,128]{1,0:T(8,128)} %get-tuple-element.5) | copy-start | bytes 86020

commit v5 on v4

--- a/solution.py
+++ b/solution.py
@@ -16,7 +16,7 @@
 SHARE = KB // 4
 MESH = pl.DeviceIdType.MESH
 ORDER = (8, 7, 9, 6, 10, 5, 11, 4, 12, 3, 13, 2, 14, 1, 15)
-GROUP = 2
+GROUP = 1
 GROUPS = 8 // GROUP
 BF = jnp.bfloat16
 F32 = jnp.float32
@@ -93,9 +93,10 @@
         rcopy(g.at[z, x, yl], g.at[z, x, yl], ss.at[0], rs.at[0], at_y)
         await_bytes(g.at[z, x, 1 - yl], rs.at[0])
 
-    def gather(g, ss, rs):
+    def gather(g, ss, rs, between):
         for d in (4, 3, 5, 2, 6, 1, 7):
             rcopy(g.at[z, x], g.at[z, x], ss.at[1], rs.at[1], at_z(d))
+        between()
         await_bytes(g.at[pl.ds(0, 7), x], rs.at[1])
         xl = lax.rem(x + 3, 4)
         xr = lax.rem(x + 1, 4)
@@ -142,14 +143,16 @@
         hand(piece, bl, 0, ss, rs)
         hand(piece, br, 1, ss, rs)
 
-    def ring_late(piece, ss, rs):
+    def ring_near(piece, ss, rs):
         bl = s * 4 + t_left
         br = s * 4 + t_right
-        bf = s * 4 + t_far
         await_bytes(piece(bl, 1), rs.at[1])
         hand(piece, bl, 1, ss, rs)
         await_bytes(piece(br, 0), rs.at[2])
         hand(piece, br, 0, ss, rs)
+
+    def ring_late(piece, ss, rs):
+        bf = s * 4 + t_far
         await_bytes(piece(bf, 0), rs.at[4])
         hand(piece, bf, 0, ss, rs)
         await_bytes(piece(bf, 1), rs.at[5])
@@ -171,7 +174,11 @@
     pcopy.start()
     gather_y(ga, g1s, g1r)
     ring_start(w_own, w_piece, w_s, w_r)
-    ring_second(w_own, w_piece, w_s, w_r)
+
+    @pl.when(s == 0)
+    def _():
+        ring_second(w_own, w_piece, w_s, w_r)
+
     wcopy = pltpu.make_async_copy(w_ref, wf.at[pl.ds(pl.multiple_of(KB * b, 64), KB), :], loc_sem.at[1])
     wcopy.start()
 
@@ -216,7 +223,7 @@
             rcopy(ph.at[pl.ds(pl.multiple_of(zo * KB, 64), KB), :], phr.at[z], p_s, p_r, at_z(d))
         phr[z] = ph[pl.ds(pl.multiple_of(z * KB, 64), KB), :]
 
-    gather(ga, g1s, g1r)
+    gather(ga, g1s, g1r, lambda: None)
     inv1 = normalize(ga)
     part = jnp.dot(proj[:, pl.ds(pl.multiple_of(s * D, D), D)], rt[...], preferred_element_type=F32)
     own_rows = pl.ds(pl.multiple_of(v * C, 8), C)
@@ -230,6 +237,7 @@
         rcopy(xch, xin, x_s.at[0], x_r.at[0], sib)
         inv_keep[...] = jnp.broadcast_to(inv1, (8, T))
         ring_mid(w_piece, w_s, w_r)
+        ring_near(w_piece, w_s, w_r)
 
     @pl.when(s == 1)
     def _():
@@ -237,21 +245,24 @@
         mixed = part + xin[pl.ds(0, C), :]
         gb[z, x, yl] = jnp.concatenate([mixed, jnp.zeros((CP - C, T), F32)], axis=0).astype(BF)
         rcopy(gb.at[z, x, yl], gb.at[z, x, yl], g2s.at[0], g2r.at[0], at_y)
+        ring_second(w_own, w_piece, w_s, w_r)
         ring_mid(w_piece, w_s, w_r)
         await_bytes(gb.at[z, x, 1 - yl], g2r.at[0])
-        gather(gb, g2s, g2r)
+        gather(gb, g2s, g2r, lambda: None)
+        ring_near(w_piece, w_s, w_r)
         inv_keep[...] = jnp.broadcast_to(normalize(gb), (8, T))
         await_bytes(phr.at[pl.ds(0, 7)], p_r)
         for i in range(4):
             pb[:, pl.ds(i * T, T)] = phr[2 * i] + phr[2 * i + 1]
 
+    ring_late(w_piece, w_s, w_r)
+
     def turn(i, carry):
         r = pl.multiple_of(i * T, T)
         rnd[:, pl.ds(r, T)] = normed[pl.ds(r, T), :].T.astype(BF)
         return carry
 
     lax.fori_loop(0, D // T, turn, 0)
-    ring_late(w_piece, w_s, w_r)
     wcopy.wait()
     await_bytes(wf.at[pl.ds(0, 4 * KB), :], w_r.at[6])
 
@@ -386,6 +397,7 @@
 
     def head_grad():
         await_bytes(r_all.at[pl.ds(0, 3 * SHARE), :], ra_r)
+        ring_near(l_piece, l_s, l_r)
         ring_late(l_piece, l_s, l_r)
         await_bytes(lg_all.at[:, pl.ds(0, 4 * T)], l_r.at[6])
 

time: 132 us -> 130 us (0.985)
  Pallas kernels: 128 us -> 126 us
    pallas_call x1, Pallas kernels: 128 us -> 126 us  [local(): pl.pallas_call(kernel, out_shape=(jax.ShapeDtypeStruct((KB, VS), BF), jax...]
where the time goes in v5:
time: 130 us
  Pallas kernels  126 us (97%)
  local copies, waits for them, and re-layouts  2.78 us (2%)
    pallas_call x1, Pallas kernels, local(): pl.pallas_call(kernel, out_shape=(jax.ShapeDtypeStruct((KB, VS), BF), jax...  126 us
    unnamed x4, local copies, waits for them, and re-layouts  2.78 us

profile of v5, /device:TPU:1, one launch (start us, length us, event | category | flops | bytes accessed | tf_op | source)
XLA Modules:
  0.0 129.6 jit_solution(5241999502959435848)
XLA Ops:
  0.6 126.1 %head.1 = (bf16[448,1024]{1,0:T(8,128)(2,1)}, f32[56,128]{1,0:T(8,128)}) custom-call(bf16[1,56,128]{2,1,0:T(8,128)(2,1)} %bitcast.5, s32[1,128]{1,0:T(1,128)} %lab_ref.1, bf16[56,7168]{1,0:T(8,128)(2,1)} %bitcast.4, bf16[448,1024]{1,0:T(8,128)(2,1)} %w_ref.1), custom_call_target="tpu_custom_call" | custom-call | flops 3000000000 | bytes 20000000 | tf_op jit(solution)/shard_map/head/pallas_call | solution.py:487
  126.8 0.0 copy-start
  126.8 2.2 %copy.8 = bf16[448,1024]{1,0:T(8,128)(2,1)} copy(bf16[448,1024]{1,0:T(8,128)(2,1)} %get-tuple-element.8) | data formatting | bytes 1835008
  128.9 0.0 copy-done
  128.9 0.6 copy.9
Async XLA Ops:
  126.8 2.2 %copy-start = (f32[56,128]{1,0:T(8,128)S(1)}, f32[56,128]{1,0:T(8,128)}, u32[]{:S(2)}) copy-start(f32[56,128]{1,0:T(8,128)} %get-tuple-element.5) | copy-start | bytes 86020

commit v6 on v5

--- a/solution.py
+++ b/solution.py
@@ -137,9 +137,11 @@
         bl = s * 4 + t_left
         br = s * 4 + t_right
         await_bytes(piece(bl, 0), rs.at[0])
-        rcopy(piece(bl, 0), piece(bl, 0), ss, rs.at[4], {"tok": t_right})
+        for q in range(2):
+            rcopy(piece(bl, 0, q), piece(bl, 0, q), ss, rs.at[4 + 3 * q], {"tok": t_right})
         await_bytes(piece(br, 1), rs.at[3])
-        rcopy(piece(br, 1), piece(br, 1), ss, rs.at[5], {"tok": t_left})
+        for q in range(2):
+            rcopy(piece(br, 1, q), piece(br, 1, q), ss, rs.at[5 + 3 * q], {"tok": t_left})
         hand(piece, bl, 0, ss, rs)
         hand(piece, br, 1, ss, rs)
 
@@ -153,19 +155,21 @@
 
     def ring_late(piece, ss, rs):
         bf = s * 4 + t_far
-        await_bytes(piece(bf, 0), rs.at[4])
-        hand(piece, bf, 0, ss, rs)
-        await_bytes(piece(bf, 1), rs.at[5])
-        hand(piece, bf, 1, ss, rs)
+        for q in range(2):
+            for h in range(2):
+                await_bytes(piece(bf, h, q), rs.at[4 + h + 3 * q])
+                rcopy(piece(bf, h, q), piece(bf, h, q), ss, rs.at[6], sib)
 
     def w_own(h):
         return w_ref.at[pl.ds(224 * h, 224), :]
 
-    def w_piece(blk, h):
-        return wf.at[pl.ds(pl.multiple_of(KB * blk + 224 * h, 32), 224), :]
-
-    def l_piece(blk, h):
-        return lg_all.at[pl.ds(512 * h, 512), pl.ds(pl.multiple_of(blk * T, T), T)]
+    def w_piece(blk, h, q=None):
+        first, count = (224 * h, 224) if q is None else (224 * h + 112 * q, 112)
+        return wf.at[pl.ds(pl.multiple_of(KB * blk + first, 16), count), :]
+
+    def l_piece(blk, h, q=None):
+        first, count = (512 * h, 512) if q is None else (512 * h + 256 * q, 256)
+        return lg_all.at[pl.ds(first, count), pl.ds(pl.multiple_of(blk * T, T), T)]
 
     def l_own(h):
         return l_piece(b, h)
@@ -203,27 +207,28 @@
         lax.fori_loop(0, 8, scale, 0)
         return inv
 
-    pcopy.wait()
-
-    @pl.when(s == 1)
-    def _():
-        odd = lax.rem(z, 2) == 1
-
-        def turn_proj(i, carry):
-            r = pl.multiple_of(i * T, T)
-            block = proj[:, pl.ds(r, T)].astype(F32)
-            even_place = jnp.concatenate([block, jnp.zeros((T - C, T), F32)], axis=0)
-            odd_place = jnp.concatenate([jnp.zeros((CP, T), F32), block, jnp.zeros((CP - C, T), F32)], axis=0)
-            ph[pl.ds(r, T), :] = jnp.where(odd, odd_place, even_place).T.astype(BF)
-            return carry
-
-        lax.fori_loop(0, D // T, turn_proj, 0)
-        for d in (4, 3, 5, 2, 6, 1, 7):
-            zo = lax.rem(z + d, 8)
-            rcopy(ph.at[pl.ds(pl.multiple_of(zo * KB, 64), KB), :], phr.at[z], p_s, p_r, at_z(d))
-        phr[z] = ph[pl.ds(pl.multiple_of(z * KB, 64), KB), :]
-
-    gather(ga, g1s, g1r, lambda: None)
+    def share_proj():
+        pcopy.wait()
+
+        @pl.when(s == 1)
+        def _():
+            odd = lax.rem(z, 2) == 1
+
+            def turn_proj(i, carry):
+                r = pl.multiple_of(i * T, T)
+                block = proj[:, pl.ds(r, T)].astype(F32)
+                even_place = jnp.concatenate([block, jnp.zeros((T - C, T), F32)], axis=0)
+                odd_place = jnp.concatenate([jnp.zeros((CP, T), F32), block, jnp.zeros((CP - C, T), F32)], axis=0)
+                ph[pl.ds(r, T), :] = jnp.where(odd, odd_place, even_place).T.astype(BF)
+                return carry
+
+            lax.fori_loop(0, D // T, turn_proj, 0)
+            for d in (4, 3, 5, 2, 6, 1, 7):
+                zo = lax.rem(z + d, 8)
+                rcopy(ph.at[pl.ds(pl.multiple_of(zo * KB, 64), KB), :], phr.at[z], p_s, p_r, at_z(d))
+            phr[z] = ph[pl.ds(pl.multiple_of(z * KB, 64), KB), :]
+
+    gather(ga, g1s, g1r, share_proj)
     inv1 = normalize(ga)
     part = jnp.dot(proj[:, pl.ds(pl.multiple_of(s * D, D), D)], rt[...], preferred_element_type=F32)
     own_rows = pl.ds(pl.multiple_of(v * C, 8), C)
@@ -336,6 +341,11 @@
     lg_all[:, pl.ds(pl.multiple_of(b * T, T), T)] = lgt
 
     ring_start(l_own, l_piece, l_s, l_r)
+
+    @pl.when(s == 0)
+    def _():
+        ring_second(l_own, l_piece, l_s, l_r)
+
     pad = jnp.zeros((CP - C, T), F32)
 
     def spread(block, p, i):
@@ -374,7 +384,10 @@
                     @pl.when(e != zy)
                     def _():
                         rcopy(az.at[e], rz.at[zy], ss2, rs2, vocab_of(e))
-        ring_second(l_own, l_piece, l_s, l_r)
+        @pl.when(s == 1)
+        def _():
+            ring_second(l_own, l_piece, l_s, l_r)
+
         ring_mid(l_piece, l_s, l_r)
         share_rows()
         await_bytes(rz.at[pl.ds(0, 15)], rs2)
@@ -517,7 +530,7 @@
             pltpu.VMEM((2 * CP, T), F32),
             pltpu.VMEM((C, T), F32),
             pltpu.VMEM((C, T), F32),
-            dma((2,)), dma, dma((7,)), dma, dma((7,)), dma, dma,
+            dma((2,)), dma, dma((9,)), dma, dma((9,)), dma, dma,
             dma((3,)), dma((6,)), dma((3,)), dma((6,)),
             dma((2,)), dma((2,)), dma((2,)), dma((9,)),
             dma, dma, dma, dma, dma, dma, dma, dma,

time: 130 us -> 129 us (level)
  no operation moved by 1% of the time
where the time goes in v6:
time: 129 us
  Pallas kernels  126 us (98%)
  local copies, waits for them, and re-layouts  2.78 us (2%)
    pallas_call x1, Pallas kernels, local(): pl.pallas_call(kernel, out_shape=(jax.ShapeDtypeStruct((KB, VS), BF), jax...  126 us
    unnamed x4, local copies, waits for them, and re-layouts  2.78 us

profile of v6, /device:TPU:1, one launch (start us, length us, event | category | flops | bytes accessed | tf_op | source)
XLA Modules:
  0.0 129.3 jit_solution(18090281513511860298)
XLA Ops:
  0.6 125.8 %head.1 = (bf16[448,1024]{1,0:T(8,128)(2,1)}, f32[56,128]{1,0:T(8,128)}) custom-call(bf16[1,56,128]{2,1,0:T(8,128)(2,1)} %bitcast.5, s32[1,128]{1,0:T(1,128)} %lab_ref.1, bf16[56,7168]{1,0:T(8,128)(2,1)} %bitcast.4, bf16[448,1024]{1,0:T(8,128)(2,1)} %w_ref.1), custom_call_target="tpu_custom_call" | custom-call | flops 3000000000 | bytes 20000000 | tf_op jit(solution)/shard_map/head/pallas_call | solution.py:500
  126.5 0.0 copy-start
  126.5 2.2 %copy.8 = bf16[448,1024]{1,0:T(8,128)(2,1)} copy(bf16[448,1024]{1,0:T(8,128)(2,1)} %get-tuple-element.8) | data formatting | bytes 1835008
  128.6 0.0 copy-done
  128.6 0.6 copy.9
Async XLA Ops:
  126.5 2.2 %copy-start = (f32[56,128]{1,0:T(8,128)S(1)}, f32[56,128]{1,0:T(8,128)}, u32[]{:S(2)}) copy-start(f32[56,128]{1,0:T(8,128)} %get-tuple-element.5) | copy-start | bytes 86020

commit v7 on v6

--- a/solution.py
+++ b/solution.py
@@ -93,11 +93,16 @@
         rcopy(g.at[z, x, yl], g.at[z, x, yl], ss.at[0], rs.at[0], at_y)
         await_bytes(g.at[z, x, 1 - yl], rs.at[0])
 
-    def gather(g, ss, rs, between):
+    def gather(g, ss, rs, between, direct=False):
         for d in (4, 3, 5, 2, 6, 1, 7):
             rcopy(g.at[z, x], g.at[z, x], ss.at[1], rs.at[1], at_z(d))
         between()
         await_bytes(g.at[pl.ds(0, 7), x], rs.at[1])
+        if direct:
+            for d in (2, 1, 3):
+                rcopy(g.at[:, x], g.at[:, x], ss.at[2], rs.at[2], at_x(d))
+            await_bytes(g.at[:, pl.ds(0, 3)], rs.at[2])
+            return
         xl = lax.rem(x + 3, 4)
         xr = lax.rem(x + 1, 4)
         rcopy(g.at[:, x], g.at[:, x], ss.at[2], rs.at[2], at_x(1))
@@ -253,7 +258,7 @@
         ring_second(w_own, w_piece, w_s, w_r)
         ring_mid(w_piece, w_s, w_r)
         await_bytes(gb.at[z, x, 1 - yl], g2r.at[0])
-        gather(gb, g2s, g2r, lambda: None)
+        gather(gb, g2s, g2r, lambda: None, direct=True)
         ring_near(w_piece, w_s, w_r)
         inv_keep[...] = jnp.broadcast_to(normalize(gb), (8, T))
         await_bytes(phr.at[pl.ds(0, 7)], p_r)

time: 129 us -> 129 us (level)
  no operation moved by 1% of the time
where the time goes in v7:
time: 129 us
  Pallas kernels  126 us (98%)
  local copies, waits for them, and re-layouts  2.78 us (2%)
    pallas_call x1, Pallas kernels, local(): pl.pallas_call(kernel, out_shape=(jax.ShapeDtypeStruct((KB, VS), BF), jax...  126 us
    unnamed x4, local copies, waits for them, and re-layouts  2.78 us

profile of v7, /device:TPU:1, one launch (start us, length us, event | category | flops | bytes accessed | tf_op | source)
XLA Modules:
  0.0 129.0 jit_solution(3832252912949276897)
XLA Ops:
  0.6 125.6 %head.1 = (bf16[448,1024]{1,0:T(8,128)(2,1)}, f32[56,128]{1,0:T(8,128)}) custom-call(bf16[1,56,128]{2,1,0:T(8,128)(2,1)} %bitcast.5, s32[1,128]{1,0:T(1,128)} %lab_ref.1, bf16[56,7168]{1,0:T(8,128)(2,1)} %bitcast.4, bf16[448,1024]{1,0:T(8,128)(2,1)} %w_ref.1), custom_call_target="tpu_custom_call" | custom-call | flops 3000000000 | bytes 20000000 | tf_op jit(solution)/shard_map/head/pallas_call | solution.py:505
  126.3 0.0 copy-start
  126.3 2.2 %copy.8 = bf16[448,1024]{1,0:T(8,128)(2,1)} copy(bf16[448,1024]{1,0:T(8,128)(2,1)} %get-tuple-element.8) | data formatting | bytes 1835008
  128.4 0.0 copy-done
  128.4 0.6 copy.9
Async XLA Ops:
  126.3 2.2 %copy-start = (f32[56,128]{1,0:T(8,128)S(1)}, f32[56,128]{1,0:T(8,128)}, u32[]{:S(2)}) copy-start(f32[56,128]{1,0:T(8,128)} %get-tuple-element.5) | copy-start | bytes 86020
